TPU v7x, 256 devices: a whole 4x4x8 slice. The times are simulated.
256 devices in a mesh: row: 16 (over x, z_lo, core), col: 16 (over y, z_hi).
Axes of the slice: x: 4, y: 4, z: 8 (z_hi: 4, z_lo: 2; z = z_hi * 2 + z_lo), core: 2. Of those that a mesh axis runs over, the one named last changes fastest.
Arguments:
- features: bfloat16 [65536, 256], P(('row', 'col')), may hold values from -6 to 6
- weight: bfloat16 [256, 256], replicated, may hold values from -0.375 to 0.375
- adjacency: bfloat16 [16, 16, 192, 128, 128], P('row', 'col'), may hold values from 0 to 0.0625
- tile_row: int32 [16, 16, 192], P('row', 'col'), may hold values from 0 to 31
- tile_col: int32 [16, 16, 192], P('row', 'col'), may hold values from 0 to 31
- tile_count: int32 [16, 16], P('row', 'col'), may hold values from 24 to 192, as said below
- cotangent: bfloat16 [65536, 256], P(('row', 'col')), may hold values from -6 to 6
Outputs:
- output: bfloat16 [65536, 256], P(('row', 'col'))
- grad_weight: float32 [256, 256], replicated
- grad_input: bfloat16 [65536, 256], P(('row', 'col'))
Inputs may be any that keep to these rules, and one draw needn't show every extreme that they name: `tile_count`: the busiest cell uses all 192 slots; the others use between 24 and 96.
All inputs are finite; a program needn't handle non-finite values.
Results may differ from a plain program's by a relative error of at most 0.0067.
Values may be sent and summed in bfloat16 or wider, within the bound.
A program may use at most 128 MiB of HBM per device.

v0:
```python
import jax
import jax.numpy as jnp
from jax import lax
from jax.sharding import PartitionSpec as P


def aggregate(slot_tiles, slot_rows, slot_cols, live_count, source, out_tiles, transposed):
    slots = slot_tiles.shape[0]
    tile_size = slot_tiles.shape[1]
    width = source.shape[1]
    blocks = source.reshape(-1, tile_size, width)
    group_size = 32
    groups = slots // group_size
    active = (jnp.arange(slots) < live_count).astype(jnp.float32)
    starts = jnp.arange(groups) * group_size

    def accumulate(running, packed):
        tile_group, row_group, col_group, active_group, start = packed

        def work(current):
            if transposed:
                products = jnp.einsum(
                    "kab,kaf->kbf",
                    tile_group,
                    blocks[row_group],
                    preferred_element_type=jnp.float32,
                )
                placed = col_group
            else:
                products = jnp.einsum(
                    "kab,kbf->kaf",
                    tile_group,
                    blocks[col_group],
                    preferred_element_type=jnp.float32,
                )
                placed = row_group
            return current.at[placed].add(products * active_group[:, None, None])

        def keep(current):
            return current

        running = lax.cond(start < live_count, work, keep, running)
        return (running, None)

    initial = jnp.zeros((out_tiles, tile_size, width), jnp.float32)
    packed = (
        slot_tiles.reshape(groups, group_size, tile_size, tile_size),
        slot_rows.reshape(groups, group_size),
        slot_cols.reshape(groups, group_size),
        active.reshape(groups, group_size),
        starts,
    )
    running, _ = lax.scan(accumulate, initial, packed)
    return running.reshape(out_tiles * tile_size, width)


def shards(features, weight, adjacency, tile_row, tile_col, tile_count, cotangent):
    local_tiles = adjacency[0, 0]
    slot_rows = tile_row[0, 0]
    slot_cols = tile_col[0, 0]
    live_count = tile_count[0, 0]
    row_devices = lax.axis_size("row")
    col_devices = lax.axis_size("col")
    owned = features.shape[0]
    tile_size = local_tiles.shape[1]
    source = lax.all_gather(features, "row", axis=0, tiled=True)
    partial_value = aggregate(
        local_tiles,
        slot_rows,
        slot_cols,
        live_count,
        source,
        col_devices * owned // tile_size,
        False,
    )
    summed = lax.psum_scatter(partial_value, "col", scatter_dimension=0, tiled=True)
    aggregated = summed.astype(jnp.bfloat16)
    preact = jnp.dot(aggregated, weight, preferred_element_type=jnp.float32)
    activated, pullback = jax.vjp(jax.nn.gelu, preact)
    delta = pullback(cotangent.astype(jnp.float32))[0].astype(jnp.bfloat16)
    back = jnp.dot(delta, weight.T, preferred_element_type=jnp.float32).astype(jnp.bfloat16)
    back_rows = lax.all_gather(back, "col", axis=0, tiled=True)
    weight_term = jnp.dot(aggregated.T, delta, preferred_element_type=jnp.float32)
    grad_weight = lax.psum(weight_term, ("row", "col"))
    spread_back = aggregate(
        local_tiles,
        slot_rows,
        slot_cols,
        live_count,
        back_rows,
        row_devices * owned // tile_size,
        True,
    )
    grad_input = lax.psum_scatter(spread_back, "row", scatter_dimension=0, tiled=True).astype(
        jnp.bfloat16
    )
    return (activated.astype(jnp.bfloat16), grad_weight, grad_input)


def solution(mesh):
    return jax.shard_map(
        shards,
        mesh=mesh,
        in_specs=(
            P(("row", "col"), None),
            P(),
            P("row", "col", None, None, None),
            P("row", "col", None),
            P("row", "col", None),
            P("row", "col"),
            P(("row", "col"), None),
        ),
        out_specs=(P(("row", "col"), None), P(), P(("row", "col"), None)),
        check_vma=False,
    )
```

profile of v0, /device:TPU:1, one launch (start us, length us, event | category | flops | bytes accessed | tf_op | source)
XLA Modules:
  0.0 758.6 jit_solution(18072197723414111471)
XLA Ops:
  11.3 39.4 %all-gather.3.cloned.1.call-done = bf16[4096,256]{1,0:T(8,128)(2,1)} async-done(((bf16[256,256]{1,0:T(8,128)(2,1)}), bf16[4096,256]{1,0:T(8,128)(2,1)}) %all-gather.3.cloned.1.call-update) | async-done | bytes 2097168 | tf_op jit(solution)/shard_map/all_gather | solution.py:66
  50.7 2.5 broadcast.88.clone
  53.2 47.8 %while.30 = (s32[]{:T(128)}, f32[32,128,256]{2,1,0:T(8,128)}, s32[6]{0:T(128)S(1)}, s32[]{:T(128)}, s32[6,32]{1,0:T(8,128)S(1)}, /*index=5*/bf16[6,32,128,128]{3...) while((s32[]{:T(128)}, f32[32,128,256]{2,1,0:T(8,128)}, ...), condition=%wide.region_4.5_spmd.clone.clone, body=%wide.region_0.4_spmd.clone.clone.sunk | while | flops 270534592 | bytes 24124100 | solution.py:53
  55.7 16.2 %conditional.8 = (f32[32,128,256]{2,1,0:T(8,128)}) conditional(s32[]{:T(128)} %convert_element_type.80, f32[32,128,256]{2,1,0:T(8,128)} %get-tuple-element.487, (s32[6,32]{1,0:T(8,128)S(1)}, s32[]{:T(128)}, bf16[6,32,128,128]{3,2,1,0:T(8,128)(2,1)}, s32[6,32]{1,0:T(8,128)S(1)}, bf16[32,128,256]{2,1,0:T(8,128)(2,1)}, /*index=5*/f32[6,32]{1,0:T(8,128)S(1)}, ...), branch_computations={%region_1.1_spmd, %region_2.3_spmd} | conditional | flops 270533824 | bytes 24123152 | solution.py:42
  55.8 2.3 gather_fusion
  58.1 3.9 convolution_multiply_fusion
  61.9 10.0 %scatter_fusion = f32[32,128,256]{2,1,0:T(8,128)} fusion(f32[32,128,256]{2,1,0:T(8,128)} %get-tuple-element.210, s32[32]{0:T(128)S(1)} %get-tuple-element.373, f32[32,128,256]{2,1,0:T(8,128)} %convolution_multiply_fusion), kind=kCustom, calls=%fused_computation.2 | custom fusion | flops 1048576 | bytes 12583040 | tf_op jit(solution)/shard_map/while/body/eval_jaxpr/cond/branch_1_fun/scatter-add | solution.py:37
  74.5 16.2 %conditional.8 = (f32[32,128,256]{2,1,0:T(8,128)}) conditional(s32[]{:T(128)} %convert_element_type.80, f32[32,128,256]{2,1,0:T(8,128)} %get-tuple-element.487, (s32[6,32]{1,0:T(8,128)S(1)}, s32[]{:T(128)}, bf16[6,32,128,128]{3,2,1,0:T(8,128)(2,1)}, s32[6,32]{1,0:T(8,128)S(1)}, bf16[32,128,256]{2,1,0:T(8,128)(2,1)}, /*index=5*/f32[6,32]{1,0:T(8,128)S(1)}, ...), branch_computations={%region_1.1_spmd, %region_2.3_spmd} | conditional | flops 270533824 | bytes 24123152 | solution.py:42
  74.5 2.3 gather_fusion
  76.8 3.9 convolution_multiply_fusion
  80.7 10.0 %scatter_fusion = f32[32,128,256]{2,1,0:T(8,128)} fusion(f32[32,128,256]{2,1,0:T(8,128)} %get-tuple-element.210, s32[32]{0:T(128)S(1)} %get-tuple-element.373, f32[32,128,256]{2,1,0:T(8,128)} %convolution_multiply_fusion), kind=kCustom, calls=%fused_computation.2 | custom fusion | flops 1048576 | bytes 12583040 | tf_op jit(solution)/shard_map/while/body/eval_jaxpr/cond/branch_1_fun/scatter-add | solution.py:37
  101.1 153.6 %reduce-scatter.3.cloned.1.call-done = f32[256,256]{1,0:T(8,128)} async-done(((f32[4096,256]{1,0:T(8,128)}), f32[256,256]{1,0:T(8,128)}) %reduce-scatter.3.cloned.1.call-update) | async-done | bytes 262160 | tf_op jit(solution)/shard_map/reduce_scatter | solution.py:76
  257.6 8.6 %copy.10 = bf16[1,1,192,128,128]{3,4,2,1,0:T(8,128)(2,1)} copy(bf16[1,1,192,128,128]{4,3,2,1,0:T(8,128)(2,1)} %bitcast.66) | data formatting | bytes 12582912 | tf_op args[2]
  266.2 49.4 %all-gather.5.cloned.1.call-done = bf16[4096,256]{1,0:T(8,128)(2,1)} async-done(((bf16[256,256]{1,0:T(8,128)(2,1)}), bf16[4096,256]{1,0:T(8,128)(2,1)}) %all-gather.5.cloned.1.call-update) | async-done | bytes 2097168 | tf_op jit(solution)/shard_map/all_gather | solution.py:82
  315.6 2.6 broadcast.88
  318.2 47.9 %while.31 = (s32[]{:T(128)}, f32[32,128,256]{2,1,0:T(8,128)}, s32[6]{0:T(128)S(1)}, s32[]{:T(128)}, s32[6,32]{1,0:T(8,128)S(1)}, /*index=5*/bf16[6,32,128,128]{2...) while((s32[]{:T(128)}, f32[32,128,256]{2,1,0:T(8,128)}, ...), condition=%wide.region_11.12_spmd.clone.clone, body=%wide.region_7.11_spmd.clone.clone.sunk | while | flops 270534592 | bytes 24124100 | solution.py:53
  320.7 16.4 %conditional.9 = (f32[32,128,256]{2,1,0:T(8,128)}) conditional(s32[]{:T(128)} %convert_element_type.82, f32[32,128,256]{2,1,0:T(8,128)} %get-tuple-element.514, (s32[6,32]{1,0:T(8,128)S(1)}, s32[]{:T(128)}, bf16[6,32,128,128]{2,3,1,0:T(8,128)(2,1)}, s32[6,32]{1,0:T(8,128)S(1)}, bf16[32,128,256]{2,1,0:T(8,128)(2,1)}, ...), branch_computations={%region_8.8_spmd, %region_9.10_spmd} | conditional | flops 270533824 | bytes 24123152 | solution.py:42
  323.1 3.9 convolution_multiply_fusion.1
  327.0 10.1 %scatter_fusion.1 = f32[32,128,256]{2,1,0:T(8,128)} fusion(f32[32,128,256]{2,1,0:T(8,128)} %get-tuple-element.227, s32[32]{0:T(128)S(1)} %get-tuple-element.375, f32[32,128,256]{2,1,0:T(8,128)} %convolution_multiply_fusion.1), kind=kCustom, calls=%fused_computation.3 | custom fusion | flops 1048576 | bytes 12583040 | tf_op jit(solution)/shard_map/while/body/eval_jaxpr/cond/branch_1_fun/scatter-add | solution.py:37
  339.6 16.1 %conditional.9 = (f32[32,128,256]{2,1,0:T(8,128)}) conditional(s32[]{:T(128)} %convert_element_type.82, f32[32,128,256]{2,1,0:T(8,128)} %get-tuple-element.514, (s32[6,32]{1,0:T(8,128)S(1)}, s32[]{:T(128)}, bf16[6,32,128,128]{2,3,1,0:T(8,128)(2,1)}, s32[6,32]{1,0:T(8,128)S(1)}, bf16[32,128,256]{2,1,0:T(8,128)(2,1)}, ...), branch_computations={%region_8.8_spmd, %region_9.10_spmd} | conditional | flops 270533824 | bytes 24123152 | solution.py:42
  342.0 3.9 convolution_multiply_fusion.1
  345.9 9.8 %scatter_fusion.1 = f32[32,128,256]{2,1,0:T(8,128)} fusion(f32[32,128,256]{2,1,0:T(8,128)} %get-tuple-element.227, s32[32]{0:T(128)S(1)} %get-tuple-element.375, f32[32,128,256]{2,1,0:T(8,128)} %convolution_multiply_fusion.1), kind=kCustom, calls=%fused_computation.3 | custom fusion | flops 1048576 | bytes 12583040 | tf_op jit(solution)/shard_map/while/body/eval_jaxpr/cond/branch_1_fun/scatter-add | solution.py:37
  367.9 126.1 %reduce-scatter.5.cloned.1.call-done = f32[256,256]{1,0:T(8,128)} async-done(((f32[4096,256]{1,0:T(8,128)}), f32[256,256]{1,0:T(8,128)}) %reduce-scatter.5.cloned.1.call-update) | async-done | bytes 262160 | tf_op jit(solution)/shard_map/reduce_scatter | solution.py:94
  495.7 254.7 %all-reduce.2.cloned.1.call-done = f32[256,256]{1,0:T(8,128)} async-done(((f32[256,256]{1,0:T(8,128)}), f32[256,256]{1,0:T(8,128)}) %all-reduce.2.cloned.1.call-update) | async-done | bytes 262160 | tf_op jit(solution)/shard_map/psum | solution.py:84
  (73 shorter events, 31.9 us)
Async XLA Ops:
  7.2 247.5 %copy-start = (bf16[256,256]{1,0:T(8,128)(2,1)S(1)}, bf16[256,256]{1,0:T(8,128)(2,1)}, u32[]{:S(2)}) copy-start(bf16[256,256]{1,0:T(8,128)(2,1)} %param.16) | copy-start | bytes 393220
  7.2 43.5 %all-gather.3.cloned.1.call-start = ((), (), s32[]{:S(2)}) async-start(), calls=%async_computation.2 | async-start | bytes 2228224 | tf_op jit(solution)/shard_map/all_gather | solution.py:66
  7.9 246.8 %reduce-scatter.3.cloned.1.call-start = ((), (), s32[]{:S(2)}) async-start(), calls=%async_computation.3 | async-start | bytes 4456448 | tf_op jit(solution)/shard_map/reduce_scatter | solution.py:76
  101.0 153.7 %copy-start.2 = (bf16[256,256]{1,0:T(8,128)(2,1)S(1)}, bf16[256,256]{1,0:T(8,128)(2,1)}, u32[]{:S(2)}) copy-start(bf16[256,256]{1,0:T(8,128)(2,1)} %param.21) | copy-start | bytes 393220
  101.1 214.6 %all-gather.5.cloned.1.call-start = ((), (), s32[]{:S(2)}) async-start(), calls=%async_computation.5 | async-start | bytes 2228224 | tf_op jit(solution)/shard_map/all_gather | solution.py:82
  257.6 236.5 %reduce-scatter.5.cloned.1.call-start = ((), (), s32[]{:S(2)}) async-start(), calls=%async_computation.6 | async-start | bytes 4456448 | tf_op jit(solution)/shard_map/reduce_scatter | solution.py:94
  366.0 1.0 copy-start.1
  366.1 384.4 %all-reduce.2.cloned.1.call-start = ((), (), s32[]{:S(2)}) async-start(), calls=%async_computation.4 | async-start | bytes 524288 | tf_op jit(solution)/shard_map/psum | solution.py:84
Sparse Core Ops, SparseCore 0:
  9.9 40.8 all-gather.2
  101.2 153.4 reduce-scatter.2
  258.0 57.5 all-gather.4
  366.2 127.8 reduce-scatter.4
  500.9 249.5 all-reduce.1
where the time goes:
time: 763 us; the launch traced here: 759 us
  waiting for transfers between devices  624 us (82%)
  other arithmetic  52.1 us (7%)
  local copies, waits for them, and re-layouts  33.1 us (4%)
  matrix products  19.4 us (3%)
  loops' own time  16.1 us (2%)
  between operations  13.8 us (2%)
    psum x1, waiting for transfers between devices, shards(): grad_weight = lax.psum(weight_term, ('row', 'col'))  255 us
    reduce_scatter x1, waiting for transfers between devices, shards(): lax.psum_scatter(partial_value, 'col', scatter_dimension=0, tiled=True)  154 us
    reduce_scatter x1, waiting for transfers between devices, shards(): lax.psum_scatter(spread_back, 'row', scatter_dimension=0, tiled=True)  126 us
    all_gather x1, waiting for transfers between devices, shards(): back_rows = lax.all_gather(back, 'col', axis=0, tiled=True)  49.4 us
    scatter-add x4, other arithmetic, work(): return current.at[placed].add(products * active_group[:, None, None])  39.9 us
    all_gather x1, waiting for transfers between devices, shards(): source = lax.all_gather(features, 'row', axis=0, tiled=True)  39.4 us
    another operation x2, loops' own time, aggregate(): running, _ = lax.scan(accumulate, initial, packed)  15.8 us
  transfers between devices with their start and end apart: 5, of which 5 were waited for; matrix products, arithmetic and copies ran while one was open for 2% of the time, Pallas kernels for 0%

commit v1 on v0

v1 whole, which is shorter than its diff:
```python
import functools
import math

import jax
import jax.numpy as jnp
from jax import lax
from jax.experimental import pallas as pl
from jax.experimental.pallas import tpu as pltpu
from jax.sharding import PartitionSpec as P

MESH = pl.DeviceIdType.MESH
BF16 = jnp.bfloat16
F32 = jnp.float32
TILE = 128
OWNED = 256
WIDTH = 256
NODES = 4096
CHUNK = 16
VMEM_LIMIT = 56 * 1024 * 1024

VMEM_SPEC = pl.BlockSpec(memory_space=pltpu.VMEM)
SMEM_SPEC = pl.BlockSpec(memory_space=pltpu.SMEM)
ANY_SPEC = pl.BlockSpec(memory_space=pl.ANY)


class Place:
    def __init__(self):
        row = lax.axis_index("row")
        col = lax.axis_index("col")
        self.x = row // 4
        self.zl = (row // 2) % 2
        self.core = row % 2
        self.y = col // 4
        self.zh = col % 4

    def at(self, dx=0, dzl=0, dcore=0, dy=0, dzh=0):
        x = (self.x + dx) % 4
        zl = (self.zl + dzl) % 2
        core = (self.core + dcore) % 2
        y = (self.y + dy) % 4
        zh = (self.zh + dzh) % 4
        return (x * 4 + zl * 2 + core, y * 4 + zh)


class Sender:
    def __init__(self, send_sems, recv_sems):
        self.send_sems = send_sems
        self.recv_sems = recv_sems
        self.used = 0
        self.started = []

    def copy(self, src, dst, device):
        made = pltpu.make_async_remote_copy(
            src_ref=src,
            dst_ref=dst,
            send_sem=self.send_sems.at[self.used],
            recv_sem=self.recv_sems.at[self.used],
            device_id=device,
            device_id_type=MESH,
        )
        made.start()
        self.used += 1
        self.started.append(made)
        return made

    def finish(self):
        for made in self.started:
            made.wait_send()


def greet(devices):
    barrier = pltpu.get_barrier_semaphore()
    for device in devices:
        pl.semaphore_signal(barrier, inc=1, device_id=device, device_id_type=MESH)
    pl.semaphore_wait(barrier, len(devices))


def rows_at(start, size):
    return pl.ds(pl.multiple_of(start, TILE), size)


def gather_kernel(features, gathered, send_sems, recv_sems):
    here = Place()
    other = here.at(dcore=1)
    across = here.at(dzl=1)
    right = here.at(dx=1)
    left = here.at(dx=-1)
    greet((other, across, right, left))
    send = Sender(send_sems, recv_sems)

    def block(dx, dzl, part=None):
        row = here.at(dx=dx, dzl=dzl)[0]
        if part is None:
            return gathered.at[rows_at(row * OWNED, OWNED), :]
        return gathered.at[rows_at(row * OWNED + part * TILE, TILE), :]

    def whole(dx, dzl, device):
        return send.copy(block(dx, dzl), block(dx, dzl), device)

    def half(dx, dzl, part, device):
        return send.copy(block(dx, dzl, part), block(dx, dzl, part), device)

    gathered[rows_at(here.at()[0] * OWNED, OWNED), :] = features[...]
    to_across = whole(0, 0, across)
    to_right = [whole(0, 0, right)]
    to_left = [whole(0, 0, left)]
    cores = [whole(0, 0, other)]
    to_across.wait_recv()
    to_right.append(whole(0, 1, right))
    to_left.append(whole(0, 1, left))
    cores.append(whole(0, 1, other))
    far = []
    for dzl in (0, 1):
        to_right[dzl].wait_recv()
        far.append(half(-1, dzl, 0, right))
        cores.append(whole(-1, dzl, other))
        to_left[dzl].wait_recv()
        far.append(half(1, dzl, 1, left))
        cores.append(whole(1, dzl, other))
    for dzl in (0, 1):
        far[2 * dzl].wait_recv()
        far[2 * dzl + 1].wait_recv()
        cores.append(whole(2, dzl, other))
    for made in cores:
        made.wait_recv()
    send.finish()


def gather_features(features):
    return pl.pallas_call(
        gather_kernel,
        out_shape=jax.ShapeDtypeStruct((NODES, WIDTH), BF16),
        in_specs=[VMEM_SPEC],
        out_specs=VMEM_SPEC,
        scratch_shapes=[
            pltpu.SemaphoreType.DMA((24,)),
            pltpu.SemaphoreType.DMA((24,)),
        ],
        compiler_params=pltpu.CompilerParams(
            collective_id=0, has_side_effects=True, vmem_limit_bytes=VMEM_LIMIT
        ),
        name="gather_features",
    )(features)


def product_kernel(transposed, count_ref, row_ref, col_ref, tiles, source, out, held, total, sems):
    live = count_ref[0]
    slots = held.shape[0]
    chunks = slots // CHUNK

    def fetch(chunk):
        part = pl.ds(chunk * CHUNK, CHUNK)
        return pltpu.make_async_copy(tiles.at[part], held.at[part], sems.at[chunk])

    for chunk in range(chunks):
        @pl.when(chunk * CHUNK < live)
        def _():
            fetch(chunk).start()

    total[...] = jnp.zeros_like(total)
    contract = 0 if transposed else 1

    def work(chunk, carry):
        @pl.when(chunk * CHUNK < live)
        def _():
            fetch(chunk).wait()
            for step in range(CHUNK):
                slot = chunk * CHUNK + step
                row = row_ref[slot]
                col = col_ref[slot]
                taken, placed = (row, col) if transposed else (col, row)
                block = source[rows_at(taken * TILE, TILE), :]
                block = jnp.where(slot < live, block, jnp.zeros_like(block))
                product = lax.dot_general(
                    held[slot],
                    block,
                    (((contract,), (0,)), ((), ())),
                    preferred_element_type=F32,
                )
                where = rows_at(placed * TILE, TILE)
                total[where, :] = total[where, :] + product

        return carry

    lax.fori_loop(0, chunks, work, 0)
    out[...] = total[...].astype(BF16)


def products(count, tile_row, tile_col, tiles, source, transposed):
    slots = tiles.shape[0]
    return pl.pallas_call(
        functools.partial(product_kernel, transposed),
        out_shape=jax.ShapeDtypeStruct((NODES, WIDTH), BF16),
        in_specs=[SMEM_SPEC, SMEM_SPEC, SMEM_SPEC, ANY_SPEC, VMEM_SPEC],
        out_specs=VMEM_SPEC,
        scratch_shapes=[
            pltpu.VMEM((slots, TILE, TILE), BF16),
            pltpu.VMEM((NODES, WIDTH), F32),
            pltpu.SemaphoreType.DMA((slots // CHUNK,)),
        ],
        compiler_params=pltpu.CompilerParams(vmem_limit_bytes=VMEM_LIMIT),
        name="products_back" if transposed else "products",
    )(count, tile_row, tile_col, tiles, source)


SLOPE = math.sqrt(2 / math.pi)


def middle_kernel(
    parts, weight, cotangent, output, back_rows, grad_weight,
    from_left, from_right, full_left, full_right, merged_right, merged_left,
    level_send, level_recv, total, term, term_core, term_across, term_x,
    term_y, term_z, chunk_sum, send_sems, recv_sems,
):
    here = Place()
    other = here.at(dcore=1)
    across = here.at(dzl=1)
    ahead = [here.at(dx=step) for step in (1, 2, 3)]
    right = here.at(dy=1)
    left = here.at(dy=-1)
    beside = [here.at(dy=step) for step in (1, 2, 3)]
    levels = [here.at(dzh=step) for step in (2, 1, 3)]
    greet([other, across] + ahead + beside + levels)
    send = Sender(send_sems, recv_sems)
    order = (2, 1, 3, 0)

    def where(dy, dzh, part=None):
        col = here.at(dy=dy, dzh=dzh)[1]
        if part is None:
            return rows_at(col * OWNED, OWNED)
        return rows_at(col * OWNED + part * TILE, TILE)

    first_right, first_left, plain_right, plain_left = {}, {}, {}, {}
    last_right, last_left, to_level = {}, {}, {}

    def first(step):
        dzh = order[step]
        first_right[step] = send.copy(parts.at[where(2, dzh, 0), :], from_left.at[step], right)
        first_left[step] = send.copy(parts.at[where(2, dzh, 1), :], from_right.at[step], left)

    def plain(step):
        dzh = order[step]
        plain_right[step] = send.copy(
            parts.at[where(1, dzh, 1), :], full_left.at[step, pl.ds(TILE, TILE), :], right
        )
        plain_left[step] = send.copy(
            parts.at[where(-1, dzh, 0), :], full_right.at[step, pl.ds(0, TILE), :], left
        )

    def merge(step):
        dzh = order[step]
        first_right[step].wait_recv()
        merged_right[step] = (
            parts[where(1, dzh, 0), :].astype(F32) + from_left[step].astype(F32)
        ).astype(BF16)
        last_right[step] = send.copy(
            merged_right.at[step], full_left.at[step, pl.ds(0, TILE), :], right
        )
        first_left[step].wait_recv()
        merged_left[step] = (
            parts[where(-1, dzh, 1), :].astype(F32) + from_right[step].astype(F32)
        ).astype(BF16)
        last_left[step] = send.copy(
            merged_left.at[step], full_right.at[step, pl.ds(TILE, TILE), :], left
        )

    def complete(step):
        dzh = order[step]
        for made in (plain_right, plain_left, last_right, last_left):
            made[step].wait_recv()
        summed = (
            parts[where(0, dzh), :].astype(F32)
            + full_left[step].astype(F32)
            + full_right[step].astype(F32)
        )
        if step < 3:
            level_send[step] = summed.astype(BF16)
            to_level[step] = send.copy(level_send.at[step], level_recv.at[step], levels[step])
        else:
            total[...] = summed

    first(0)
    plain(0)
    first(1)
    for step in range(4):
        merge(step)
        if step < 2:
            first(step + 2)
        if step < 3:
            plain(step + 1)
        if step:
            complete(step - 1)
    complete(3)
    for step in range(3):
        to_level[step].wait_recv()
    aggregated = (
        total[...]
        + level_recv[0].astype(F32)
        + level_recv[1].astype(F32)
        + level_recv[2].astype(F32)
    ).astype(BF16)

    preact = jnp.dot(aggregated, weight[...], preferred_element_type=F32)
    squared = preact * preact
    bent = jnp.tanh(SLOPE * (preact + 0.044715 * (preact * squared)))
    output[...] = (0.5 * preact * (1.0 + bent)).astype(BF16)
    slope = 0.5 * (1.0 + bent) + 0.5 * preact * (1.0 - bent * bent) * (
        SLOPE * (1.0 + 3 * 0.044715 * squared)
    )
    delta = (cotangent[...].astype(F32) * slope).astype(BF16)
    back = lax.dot_general(
        delta, weight[...], (((1,), (1,)), ((), ())), preferred_element_type=F32
    ).astype(BF16)
    back_rows[where(0, 0), :] = back

    def spread(dy, dzh, device, part=None):
        block = back_rows.at[where(dy, dzh, part), :]
        return send.copy(block, block, device)

    up = [spread(0, 0, levels[1]), spread(0, 0, levels[2]), spread(0, 0, levels[0])]
    came = (3, 1, 2)
    ring_right = [spread(0, 0, right)]
    ring_left = [spread(0, 0, left)]
    halves = []

    def relay(step, dzh):
        ring_right[step].wait_recv()
        halves.append(spread(-1, dzh, right, 0))
        ring_left[step].wait_recv()
        halves.append(spread(1, dzh, left, 1))

    term[...] = lax.dot_general(
        aggregated, delta, (((0,), (0,)), ((), ())), preferred_element_type=F32
    )
    half_mine = here.core * 128
    half_other = 128 - half_mine
    to_core = send.copy(
        term.at[pl.ds(pl.multiple_of(half_other, 128), 128), :], term_core, other
    )

    for step in range(3):
        up[step].wait_recv()
        ring_right.append(spread(0, came[step], right))
        ring_left.append(spread(0, came[step], left))
        if step == 0:
            to_core.wait_recv()
            mine = pl.ds(pl.multiple_of(half_mine, 128), 128)
            term[mine, :] = term[mine, :] + term_core[...]
            quarter_mine = half_mine + here.zl * 64
            quarter_other = half_mine + 64 - here.zl * 64
            to_across = send.copy(
                term.at[pl.ds(pl.multiple_of(quarter_other, 64), 64), :], term_across, across
            )
        if step == 1:
            to_across.wait_recv()
            mine = pl.ds(pl.multiple_of(quarter_mine, 64), 64)
            term[mine, :] = term[mine, :] + term_across[...]
            to_x = []
            for dx in (1, 2, 3):
                piece = quarter_mine + ((here.x + dx) % 4) * 16
                to_x.append(
                    send.copy(
                        term.at[pl.ds(pl.multiple_of(piece, 16), 16), :],
                        term_x.at[dx - 1],
                        ahead[dx - 1],
                    )
                )

    relay(0, 0)
    for made in to_x:
        made.wait_recv()
    piece = pl.ds(pl.multiple_of(quarter_mine + here.x * 16, 16), 16)
    chunk_sum[0] = term[piece, :] + term_x[0] + term_x[1] + term_x[2]
    to_y = [send.copy(chunk_sum.at[0], term_y.at[dy - 1], beside[dy - 1]) for dy in (1, 2, 3)]
    relay(1, came[0])
    for made in to_y:
        made.wait_recv()
    chunk_sum[1] = (chunk_sum[0] + term_y[1]) + (term_y[0] + term_y[2])
    to_z = [send.copy(chunk_sum.at[1], term_z.at[slot], levels[slot]) for slot in range(3)]
    relay(2, came[1])
    for made in to_z:
        made.wait_recv()
    chunk_sum[2] = (chunk_sum[1] + term_z[0]) + (term_z[1] + term_z[2])
    grad_weight[piece, :] = chunk_sum[2]
    all_x = [
        send.copy(grad_weight.at[piece, :], grad_weight.at[piece, :], ahead[dx]) for dx in range(3)
    ]
    relay(3, came[2])
    for made in all_x:
        made.wait_recv()
    quarter = grad_weight.at[pl.ds(pl.multiple_of(quarter_mine, 64), 64), :]
    all_across = send.copy(quarter, quarter, across)
    halves[0].wait_recv()
    halves[1].wait_recv()
    halves[2].wait_recv()
    halves[3].wait_recv()
    all_across.wait_recv()
    half = grad_weight.at[pl.ds(pl.multiple_of(half_mine, 128), 128), :]
    all_core = send.copy(half, half, other)
    for made in halves[4:]:
        made.wait_recv()
    all_core.wait_recv()
    send.finish()


def middle(parts, weight, cotangent):
    block = (TILE, WIDTH)
    full = (OWNED, WIDTH)
    return pl.pallas_call(
        middle_kernel,
        out_shape=(
            jax.ShapeDtypeStruct((OWNED, WIDTH), BF16),
            jax.ShapeDtypeStruct((NODES, WIDTH), BF16),
            jax.ShapeDtypeStruct((WIDTH, WIDTH), F32),
        ),
        in_specs=[VMEM_SPEC] * 3,
        out_specs=(VMEM_SPEC,) * 3,
        scratch_shapes=[
            pltpu.VMEM((4,) + block, BF16),
            pltpu.VMEM((4,) + block, BF16),
            pltpu.VMEM((4,) + full, BF16),
            pltpu.VMEM((4,) + full, BF16),
            pltpu.VMEM((4,) + block, BF16),
            pltpu.VMEM((4,) + block, BF16),
            pltpu.VMEM((3,) + full, BF16),
            pltpu.VMEM((3,) + full, BF16),
            pltpu.VMEM(full, F32),
            pltpu.VMEM((WIDTH, WIDTH), F32),
            pltpu.VMEM((128, WIDTH), F32),
            pltpu.VMEM((64, WIDTH), F32),
            pltpu.VMEM((3, 16, WIDTH), F32),
            pltpu.VMEM((3, 16, WIDTH), F32),
            pltpu.VMEM((3, 16, WIDTH), F32),
            pltpu.VMEM((3, 16, WIDTH), F32),
            pltpu.SemaphoreType.DMA((64,)),
            pltpu.SemaphoreType.DMA((64,)),
        ],
        compiler_params=pltpu.CompilerParams(
            collective_id=1, has_side_effects=True, vmem_limit_bytes=VMEM_LIMIT
        ),
        name="middle",
    )(parts, weight, cotangent)


def scatter_kernel(
    parts, out, core_recv, merged, from_left, from_right, full_left, full_right,
    merged_right, merged_left, level_send, level_recv, send_sems, recv_sems,
):
    here = Place()
    other = here.at(dcore=1)
    across = here.at(dzl=1)
    right = here.at(dx=1)
    left = here.at(dx=-1)
    greet((other, across, right, left))
    send = Sender(send_sems, recv_sems)

    def where(dx, dzl, dcore=0):
        return rows_at(here.at(dx=dx, dzl=dzl, dcore=dcore)[0] * OWNED, OWNED)

    dests = [(dx, dzl) for dzl in (1, 0) for dx in (2, 1, 3, 0)]
    to_core = [
        send.copy(parts.at[where(dx, dzl, 1), :], core_recv.at[slot], other)
        for slot, (dx, dzl) in enumerate(dests)
    ]

    def collect(slot):
        to_core[slot].wait_recv()
        dx, dzl = dests[slot]
        return parts[where(dx, dzl), :].astype(F32) + core_recv[slot].astype(F32)

    low = pl.ds(0, TILE)
    high = pl.ds(TILE, TILE)
    first_right, first_left, plain_right, plain_left = {}, {}, {}, {}
    for step in range(2):
        base = 4 * step
        merged[base] = collect(base).astype(BF16)
        first_right[step] = send.copy(merged.at[base, low, :], from_left.at[step], right)
        first_left[step] = send.copy(merged.at[base, high, :], from_right.at[step], left)
        merged[base + 1] = collect(base + 1).astype(BF16)
        plain_right[step] = send.copy(
            merged.at[base + 1, high, :], full_left.at[step, high, :], right
        )
        merged[base + 2] = collect(base + 2).astype(BF16)
        plain_left[step] = send.copy(merged.at[base + 2, low, :], full_right.at[step, low, :], left)
    last_right, last_left = {}, {}
    for step in range(2):
        base = 4 * step
        first_right[step].wait_recv()
        merged_right[step] = (
            merged[base + 1, low, :].astype(F32) + from_left[step].astype(F32)
        ).astype(BF16)
        last_right[step] = send.copy(merged_right.at[step], full_left.at[step, low, :], right)
        first_left[step].wait_recv()
        merged_left[step] = (
            merged[base + 2, high, :].astype(F32) + from_right[step].astype(F32)
        ).astype(BF16)
        last_left[step] = send.copy(merged_left.at[step], full_right.at[step, high, :], left)
    for step in range(2):
        own = collect(4 * step + 3)
        for made in (plain_right, plain_left, last_right, last_left):
            made[step].wait_recv()
        summed = own + full_left[step].astype(F32) + full_right[step].astype(F32)
        if step == 0:
            level_send[...] = summed.astype(BF16)
            to_across = send.copy(level_send, level_recv, across)
        else:
            to_across.wait_recv()
            out[...] = (summed + level_recv[...].astype(F32)).astype(BF16)
    send.finish()


def scatter(parts):
    block = (TILE, WIDTH)
    full = (OWNED, WIDTH)
    return pl.pallas_call(
        scatter_kernel,
        out_shape=jax.ShapeDtypeStruct(full, BF16),
        in_specs=[VMEM_SPEC],
        out_specs=VMEM_SPEC,
        scratch_shapes=[
            pltpu.VMEM((8,) + full, BF16),
            pltpu.VMEM((8,) + full, BF16),
            pltpu.VMEM((2,) + block, BF16),
            pltpu.VMEM((2,) + block, BF16),
            pltpu.VMEM((2,) + full, BF16),
            pltpu.VMEM((2,) + full, BF16),
            pltpu.VMEM((2,) + block, BF16),
            pltpu.VMEM((2,) + block, BF16),
            pltpu.VMEM(full, BF16),
            pltpu.VMEM(full, BF16),
            pltpu.SemaphoreType.DMA((24,)),
            pltpu.SemaphoreType.DMA((24,)),
        ],
        compiler_params=pltpu.CompilerParams(
            collective_id=2, has_side_effects=True, vmem_limit_bytes=VMEM_LIMIT
        ),
        name="scatter",
    )(parts)


def shards(features, weight, adjacency, tile_row, tile_col, tile_count, cotangent):
    tiles = adjacency[0, 0]
    slot_rows = tile_row[0, 0]
    slot_cols = tile_col[0, 0]
    count = tile_count[0]
    source = gather_features(features)
    parts = products(count, slot_rows, slot_cols, tiles, source, False)
    output, back_rows, grad_weight = middle(parts, weight, cotangent)
    parts_back = products(count, slot_rows, slot_cols, tiles, back_rows, True)
    grad_input = scatter(parts_back)
    return output, grad_weight, grad_input


def solution(mesh):
    return jax.shard_map(
        shards,
        mesh=mesh,
        in_specs=(
            P(("row", "col"), None),
            P(),
            P("row", "col", None, None, None),
            P("row", "col", None),
            P("row", "col", None),
            P("row", "col"),
            P(("row", "col"), None),
        ),
        out_specs=(P(("row", "col"), None), P(), P(("row", "col"), None)),
        check_vma=False,
    )
```

time: 763 us -> 132 us (0.17)
  waiting for transfers between devices: 624 us -> 0 us
  Pallas kernels: 0 us -> 127 us
  other arithmetic: 52.1 us -> 0 us
  local copies, waits for them, and re-layouts: 33.1 us -> 2.94 us
  matrix products: 19.4 us -> 0 us
  loops' own time: 16.1 us -> 0 us
  between operations: 13.8 us -> 1.34 us
    reduce_scatter x2 -> x0, waiting for transfers between devices: 280 us -> none  [the longest x1 154 us: shards(): lax.psum_scatter(partial_value, 'col', scatter_dimension=0, tiled=True)]
    psum x1 -> x0, waiting for transfers between devices: 255 us -> none  [shards(): grad_weight = lax.psum(weight_term, ('row', 'col'))]
    pallas_call x0 -> x5, Pallas kernels: none -> 127 us  [the longest x1 71.8 us: middle(): pl.pallas_call(middle_kernel, out_shape=(jax.ShapeDtypeStruct((OWNED, WID...]
    all_gather x2 -> x0, waiting for transfers between devices: 88.8 us -> none  [the longest x1 49.4 us: shards(): back_rows = lax.all_gather(back, 'col', axis=0, tiled=True)]
    scatter-add x4 -> x0, other arithmetic: 39.9 us -> none  [work(): return current.at[placed].add(products * active_group[:, None, None])]
    dot_general x7 -> x0, matrix products: 19.4 us -> none  [the longest x2 7.89 us: work(): jnp.einsum('kab,kaf->kbf', tile_group, blocks[row_group], preferred_eleme...]
    another operation x14 -> x0, loops' own time: 16.1 us -> none  [the longest x2 15.8 us: aggregate(): running, _ = lax.scan(accumulate, initial, packed)]
    convert_element_type x13 -> x0, other arithmetic: 9.44 us -> none  [the longest x12 7.82 us: aggregate(): active = (jnp.arange(slots) < live_count).astype(jnp.float32)]
  transfers between devices with their start and end apart: 5 -> 0, of which waited for: 5 -> 0; matrix products, arithmetic and copies ran while one was open for 2% -> 0% of each run, Pallas kernels for 0% -> 0%
where the time goes in v1:
time: 132 us; the launch traced here: 131 us
  Pallas kernels  127 us (96%)
  local copies, waits for them, and re-layouts  2.94 us (2%)
  between operations  1.34 us (1%)
    pallas_call x1, Pallas kernels, middle(): pl.pallas_call(middle_kernel, out_shape=(jax.ShapeDtypeStruct((OWNED, WID...  71.8 us
    pallas_call x1, Pallas kernels, gather_features(): pl.pallas_call(gather_kernel, out_shape=jax.ShapeDtypeStruct((NODES, WIDT...  21.2 us
    pallas_call x1, Pallas kernels, scatter(): pl.pallas_call(scatter_kernel, out_shape=jax.ShapeDtypeStruct(full, BF16)...  18.7 us
    pallas_call x2, Pallas kernels, products(): pl.pallas_call(functools.partial(product_kernel, transposed), out_shape=j...  15 us
    unnamed x7, local copies, waits for them, and re-layouts  2.94 us

profile of v1, /device:TPU:1, one launch (start us, length us, event | category | flops | bytes accessed | tf_op | source)
XLA Modules:
  0.0 131.0 jit_solution(6193897303653450188)
XLA Ops:
  1.3 21.2 %gather_features.1.source = bf16[4096,256]{1,0:T(8,128)(2,1)} custom-call(bf16[256,256]{1,0:T(8,128)(2,1)} %features.1), custom_call_target="tpu_custom_call" | custom-call | tf_op jit(solution)/shard_map/gather_features/pallas_call | solution.py:130
  22.5 7.4 %products.1.parts = bf16[4096,256]{1,0:T(8,128)(2,1)} custom-call(s32[1]{0:T(128)} %bitcast.4.count_ref, s32[192]{0:T(256)} %bitcast.8, s32[192]{0:T(256)} %bitcast.10, bf16[192,128,128]{2,1,0:T(8,128)(2,1)} %bitcast.6, bf16[4096,256]{1,0:T(8,128)(2,1)} %gather_features.1.source), custom_call_target="tpu_custom_call" | custom-call | tf_op jit(solution)/shard_map/products/pallas_call | solution.py:191
  29.9 71.8 %middle.1 = (bf16[256,256]{1,0:T(8,128)(2,1)}, bf16[4096,256]{1,0:T(8,128)(2,1)}, f32[256,256]{1,0:T(8,128)}) custom-call(bf16[4096,256]{1,0:T(8,128)(2,1)} %products.1.parts, bf16[256,256]{1,0:T(8,128)(2,1)} %weight.1, bf16[256,256]{1,0:T(8,128)(2,1)} %cotangent.1), custom_call_target="tpu_custom_call" | custom-call | tf_op jit(solution)/shard_map/middle/pallas_call | solution.py:409
  101.7 7.6 %products_back.1.parts = bf16[4096,256]{1,0:T(8,128)(2,1)} custom-call(s32[1]{0:T(128)} %bitcast.5.count_ref, s32[192]{0:T(256)} %bitcast.9, s32[192]{0:T(256)} %bitcast.11, bf16[192,128,128]{2,1,0:T(8,128)(2,1)} %bitcast.7, bf16[4096,256]{1,0:T(8,128)(2,1)} %get-tuple-element.8.source), custom_call_target="tpu_custom_call" | custom-call | tf_op jit(solution)/shard_map/products_back/pallas_call | solution.py:191
  109.3 0.0 copy-start.1
  109.3 0.0 copy-start
  109.3 18.7 %scatter.1 = bf16[256,256]{1,0:T(8,128)(2,1)} custom-call(bf16[4096,256]{1,0:T(8,128)(2,1)} %products_back.1.parts), custom_call_target="tpu_custom_call" | custom-call | tf_op jit(solution)/shard_map/scatter/pallas_call | solution.py:515
  128.1 0.0 copy-done.1
  128.1 0.7 copy.14
  128.7 0.0 copy-done
  128.7 0.7 copy.15
  129.4 1.6 %copy.16 = bf16[256,256]{1,0:T(8,128)(2,1)} copy(bf16[256,256]{1,0:T(8,128)(2,1)} %scatter.1) | data formatting | bytes 262144
Async XLA Ops:
  109.3 18.8 %copy-start.1 = (bf16[256,256]{1,0:T(8,128)(2,1)S(1)}, bf16[256,256]{1,0:T(8,128)(2,1)}, u32[]{:S(2)}) copy-start(bf16[256,256]{1,0:T(8,128)(2,1)} %get-tuple-element.12) | copy-start | bytes 393220
  109.3 19.4 %copy-start = (f32[256,256]{1,0:T(8,128)S(1)}, f32[256,256]{1,0:T(8,128)}, u32[]{:S(2)}) copy-start(f32[256,256]{1,0:T(8,128)} %get-tuple-element.13) | copy-start | bytes 786436

commit v2 on v0

v2 whole, which is shorter than its diff:
```python
import functools
import math

import jax
import jax.numpy as jnp
from jax import lax
from jax.experimental import pallas as pl
from jax.experimental.pallas import tpu as pltpu
from jax.sharding import PartitionSpec as P

MESH = pl.DeviceIdType.MESH
BF16 = jnp.bfloat16
F32 = jnp.float32
TILE = 128
OWNED = 256
WIDTH = 256
HALF = 128
NODES = 4096
TILES = NODES // TILE
GROUP = 16
COPIES = 256
VMEM_LIMIT = 58 * 1024 * 1024
SLOPE = math.sqrt(2 / math.pi)

VMEM_SPEC = pl.BlockSpec(memory_space=pltpu.VMEM)
SMEM_SPEC = pl.BlockSpec(memory_space=pltpu.SMEM)
ANY_SPEC = pl.BlockSpec(memory_space=pl.ANY)
LOW = pl.ds(0, TILE)
HIGH = pl.ds(TILE, TILE)


def arrange(placed, taken, live):
    slots = placed.shape[1]
    lane = lax.broadcasted_iota(jnp.int32, (slots, slots), 1)
    line = lax.broadcasted_iota(jnp.int32, (slots, slots), 0)

    def turned(flat):
        return jnp.sum(jnp.where(lane == line, flat, 0), axis=1, keepdims=True)

    lane_row = lax.broadcasted_iota(jnp.int32, (1, slots), 1)
    tagged = jnp.where(lane_row < live, placed, TILES)
    key = tagged * 256 + lane_row
    rank = jnp.sum(jnp.where(key < turned(key), 1, 0), axis=1, keepdims=True)
    tag_line = turned(tagged)
    taken_line = turned(taken)
    chosen = rank == lane

    def pick(column):
        return jnp.sum(jnp.where(chosen, column, 0), axis=0, keepdims=True)

    order = pick(line)
    source = pick(taken_line)
    tag = pick(tag_line + 1)
    before = jnp.sum(jnp.where(rank + 1 == lane, tag_line + 1, 0), axis=0, keepdims=True)
    keep = jnp.where(tag == before, 1, 0)
    up_to = jnp.sum(jnp.where(tag_line <= lane, 1, 0), axis=0, keepdims=True)
    here = jnp.sum(jnp.where(tag_line == lane, 1, 0), axis=0, keepdims=True)
    last = jnp.where(here > 0, up_to - 1, slots)
    return (order, source, keep, last)


def order_kernel(count_ref, row_ref, col_ref, out):
    live = count_ref[0]
    rows = row_ref[...]
    cols = col_ref[...]
    found = arrange(rows, cols, live) + arrange(cols, rows, live)
    for line, value in enumerate(found):
        out[line : line + 1, :] = value


def order_slots(count, tile_row, tile_col):
    slots = tile_row.shape[1]
    return pl.pallas_call(
        order_kernel,
        out_shape=jax.ShapeDtypeStruct((8, slots), jnp.int32),
        in_specs=[SMEM_SPEC, VMEM_SPEC, VMEM_SPEC],
        out_specs=VMEM_SPEC,
        name="order_slots",
    )(count, tile_row, tile_col)


class Place:
    def __init__(self):
        row = lax.axis_index("row")
        col = lax.axis_index("col")
        self.x = row // 4
        self.zl = (row // 2) % 2
        self.core = row % 2
        self.y = col // 4
        self.zh = col % 4

    def at(self, dx=0, dzl=0, dcore=0, dy=0, dzh=0):
        x = (self.x + dx) % 4
        zl = (self.zl + dzl) % 2
        core = (self.core + dcore) % 2
        y = (self.y + dy) % 4
        zh = (self.zh + dzh) % 4
        return (x * 4 + zl * 2 + core, y * 4 + zh)


class Copy:
    def __init__(self, describe):
        self.describe = describe

    def wait_recv(self):
        self.describe().wait_recv()

    def wait_send(self):
        self.describe().wait_send()


class Sender:
    def __init__(self, send_sems, recv_sems):
        self.send_sems = send_sems
        self.recv_sems = recv_sems
        self.started = []

    def copy(self, ends, device):
        used = len(self.started)

        def describe():
            src, dst = ends()
            return pltpu.make_async_remote_copy(
                src_ref=src,
                dst_ref=dst,
                send_sem=self.send_sems.at[used],
                recv_sem=self.recv_sems.at[used],
                device_id=device,
                device_id_type=MESH,
            )

        describe().start()
        made = Copy(describe)
        self.started.append(made)
        return made

    def finish(self):
        for made in self.started:
            made.wait_send()


def greet(devices):
    barrier = pltpu.get_barrier_semaphore()
    for device in devices:
        pl.semaphore_signal(barrier, inc=1, device_id=device, device_id_type=MESH)
    pl.semaphore_wait(barrier, len(devices))


def rows_at(start, size):
    return pl.ds(pl.multiple_of(start, TILE), size)


class Around:
    def __init__(self, here):
        self.here = here
        self.other = here.at(dcore=1)
        self.across = here.at(dzl=1)
        self.ahead = [here.at(dx=step) for step in (1, 2, 3)]
        self.beside = [here.at(dy=step) for step in (1, 2, 3)]
        self.levels = [here.at(dzh=step) for step in (2, 1, 3)]

    def everyone(self):
        return [self.other, self.across] + self.ahead + self.beside + self.levels


def gather_steps(around, send, gathered):
    here = around.here
    right, left = around.ahead[0], around.ahead[2]
    to_right, to_left, cores, far = [], [], [], []
    state = {}

    def block(dx, dzl, part=None):
        row = here.at(dx=dx, dzl=dzl)[0]
        if part is None:
            return gathered.at[pl.ds(row * 2, 2)]
        return gathered.at[row * 2 + part]

    def move(dx, dzl, device, part=None):
        return send.copy(lambda dx=dx, dzl=dzl: (block(dx, dzl, part), block(dx, dzl, part)), device)

    def begin():
        state["across"] = move(0, 0, around.across)
        to_right.append(move(0, 0, right))
        to_left.append(move(0, 0, left))
        cores.append(move(0, 0, around.other))

    def second():
        state["across"].wait_recv()
        to_right.append(move(0, 1, right))
        to_left.append(move(0, 1, left))
        cores.append(move(0, 1, around.other))

    def relay(dzl):
        to_right[dzl].wait_recv()
        far.append(move(-1, dzl, right, 0))
        cores.append(move(-1, dzl, around.other))
        to_left[dzl].wait_recv()
        far.append(move(1, dzl, left, 1))
        cores.append(move(1, dzl, around.other))

    def last(dzl):
        far[2 * dzl].wait_recv()
        far[2 * dzl + 1].wait_recv()
        cores.append(move(2, dzl, around.other))

    def end():
        for made in cores:
            made.wait_recv()

    return [
        begin,
        second,
        functools.partial(relay, 0),
        functools.partial(relay, 1),
        functools.partial(last, 0),
        functools.partial(last, 1),
        end,
    ]


def reduce_steps(
    around, send, parts, from_left, from_right, full_left, full_right,
    merged_right, merged_left, level_send, level_recv, total, result,
):
    here = around.here
    right, left = around.beside[0], around.beside[2]
    order = (2, 1, 3, 0)
    first_right, first_left, plain_right, plain_left = {}, {}, {}, {}
    last_right, last_left, to_level = {}, {}, {}

    def where(dy, dzh, part=None):
        col = here.at(dy=dy, dzh=dzh)[1]
        if part is None:
            return rows_at(col * OWNED, OWNED)
        return rows_at(col * OWNED + part * TILE, TILE)

    def first(step):
        dzh = order[step]
        first_right[step] = send.copy(lambda step=step, dzh=dzh: (parts.at[where(2, dzh, 0), :], from_left.at[step]), right)
        first_left[step] = send.copy(lambda step=step, dzh=dzh: (parts.at[where(2, dzh, 1), :], from_right.at[step]), left)

    def plain(step):
        dzh = order[step]
        plain_right[step] = send.copy(lambda step=step, dzh=dzh: (parts.at[where(1, dzh, 1), :], full_left.at[step, HIGH, :]), right)
        plain_left[step] = send.copy(lambda step=step, dzh=dzh: (parts.at[where(-1, dzh, 0), :], full_right.at[step, LOW, :]), left)

    def merge(step):
        dzh = order[step]
        first_right[step].wait_recv()
        merged_right[step] = (
            parts[where(1, dzh, 0), :].astype(F32) + from_left[step].astype(F32)
        ).astype(BF16)
        last_right[step] = send.copy(lambda step=step: (merged_right.at[step], full_left.at[step, LOW, :]), right)
        first_left[step].wait_recv()
        merged_left[step] = (
            parts[where(-1, dzh, 1), :].astype(F32) + from_right[step].astype(F32)
        ).astype(BF16)
        last_left[step] = send.copy(lambda step=step: (merged_left.at[step], full_right.at[step, HIGH, :]), left)

    def complete(step):
        dzh = order[step]
        for made in (plain_right, plain_left, last_right, last_left):
            made[step].wait_recv()
        summed = (
            parts[where(0, dzh), :].astype(F32)
            + full_left[step].astype(F32)
            + full_right[step].astype(F32)
        )
        if step < 3:
            level_send[step] = summed.astype(BF16)
            to_level[step] = send.copy(lambda step=step: (level_send.at[step], level_recv.at[step]), around.levels[step])
        else:
            total[...] = summed

    def begin():
        first(0)
        plain(0)
        first(1)

    def middle(step):
        merge(step)
        if step < 2:
            first(step + 2)
        if step < 3:
            plain(step + 1)
        if step:
            complete(step - 1)

    def end():
        for step in range(3):
            to_level[step].wait_recv()
        result[...] = (
            total[...]
            + level_recv[0].astype(F32)
            + level_recv[1].astype(F32)
            + level_recv[2].astype(F32)
        ).astype(BF16)

    return (
        [begin]
        + [functools.partial(middle, step) for step in range(4)]
        + [functools.partial(complete, 3), end]
    )


def spread_steps(around, send, gathered):
    here = around.here
    right, left = around.beside[0], around.beside[2]
    ring_right, ring_left, halves = [], [], []
    up = {}
    came = {1: 3, 2: 1, 0: 2}
    rounds = [0, 3, 1, 2]

    def block(dy, dzh, part):
        col = here.at(dy=dy, dzh=dzh)[1]
        if part is None:
            return gathered.at[pl.ds(col * 2, 2)]
        return gathered.at[col * 2 + part]

    def move(dy, dzh, device, part=None):
        return send.copy(lambda: (block(dy, dzh, part), block(dy, dzh, part)), device)

    def ring(dzh):
        ring_right.append(move(0, dzh, right))
        ring_left.append(move(0, dzh, left))

    def begin():
        up[1] = move(0, 0, around.levels[1])
        up[2] = move(0, 0, around.levels[2])
        ring(0)

    def far():
        up[0] = move(0, 0, around.levels[0])

    def level(slot):
        up[slot].wait_recv()
        ring(came[slot])

    def relay(step):
        dzh = rounds[step]
        ring_right[step].wait_recv()
        halves.append(move(-1, dzh, right, 0))
        ring_left[step].wait_recv()
        halves.append(move(1, dzh, left, 1))

    def end():
        for made in halves:
            made.wait_recv()

    return {
        "begin": begin,
        "far": far,
        "level1": functools.partial(level, 1),
        "level2": functools.partial(level, 2),
        "level0": functools.partial(level, 0),
        "relay0": functools.partial(relay, 0),
        "relay1": functools.partial(relay, 1),
        "relay2": functools.partial(relay, 2),
        "relay3": functools.partial(relay, 3),
        "end": end,
    }


def scatter_steps(
    around, send, parts, out, core_recv, merged, from_left, from_right,
    full_left, full_right, merged_right, merged_left, level_send, level_recv,
):
    here = around.here
    right, left = around.ahead[0], around.ahead[2]
    dests = [(dx, dzl) for dzl in (1, 0) for dx in (2, 1, 3, 0)]
    to_core = []
    first_right, first_left, plain_right, plain_left = {}, {}, {}, {}
    last_right, last_left, state = {}, {}, {}

    def where(dx, dzl, dcore=0):
        return rows_at(here.at(dx=dx, dzl=dzl, dcore=dcore)[0] * OWNED, OWNED)

    def begin():
        for slot, (dx, dzl) in enumerate(dests):
            to_core.append(
                send.copy(lambda slot=slot, dx=dx, dzl=dzl: (parts.at[where(dx, dzl, 1), :], core_recv.at[slot]), around.other)
            )

    def collect(slot):
        to_core[slot].wait_recv()
        dx, dzl = dests[slot]
        return parts[where(dx, dzl), :].astype(F32) + core_recv[slot].astype(F32)

    def first(step):
        base = 4 * step
        merged[base] = collect(base).astype(BF16)
        first_right[step] = send.copy(lambda step=step: (merged.at[base, LOW, :], from_left.at[step]), right)
        first_left[step] = send.copy(lambda step=step: (merged.at[base, HIGH, :], from_right.at[step]), left)
        merged[base + 1] = collect(base + 1).astype(BF16)
        plain_right[step] = send.copy(lambda step=step: (merged.at[base + 1, HIGH, :], full_left.at[step, HIGH, :]), right)
        merged[base + 2] = collect(base + 2).astype(BF16)
        plain_left[step] = send.copy(lambda step=step: (merged.at[base + 2, LOW, :], full_right.at[step, LOW, :]), left)

    def last(step):
        base = 4 * step
        first_right[step].wait_recv()
        merged_right[step] = (
            merged[base + 1, LOW, :].astype(F32) + from_left[step].astype(F32)
        ).astype(BF16)
        last_right[step] = send.copy(lambda step=step: (merged_right.at[step], full_left.at[step, LOW, :]), right)
        first_left[step].wait_recv()
        merged_left[step] = (
            merged[base + 2, HIGH, :].astype(F32) + from_right[step].astype(F32)
        ).astype(BF16)
        last_left[step] = send.copy(lambda step=step: (merged_left.at[step], full_right.at[step, HIGH, :]), left)

    def complete(step):
        own = collect(4 * step + 3)
        for made in (plain_right, plain_left, last_right, last_left):
            made[step].wait_recv()
        summed = own + full_left[step].astype(F32) + full_right[step].astype(F32)
        if step == 0:
            level_send[...] = summed.astype(BF16)
            state["across"] = send.copy(lambda: (level_send, level_recv), around.across)
        else:
            state["across"].wait_recv()
            out[...] = (summed + level_recv[...].astype(F32)).astype(BF16)

    return [begin] + [
        functools.partial(step, number) for step in (first, last, complete) for number in (0, 1)
    ]


def weight_steps(
    around, send, term, grad_weight, term_core, term_across, term_x, term_y, term_z, chunk_sum
):
    here = around.here
    half_mine = here.core * 128
    half_other = 128 - half_mine
    quarter_mine = half_mine + here.zl * 64
    quarter_other = half_mine + 64 - here.zl * 64
    piece_mine = quarter_mine + here.x * 16
    state = {}

    def lines(start, size):
        return pl.ds(pl.multiple_of(start, size), size)

    def same(start, size, device):
        def ends():
            block = grad_weight.at[lines(start, size), :]
            return block, block

        return send.copy(ends, device)

    def core():
        state["core"] = send.copy(lambda: (term.at[lines(half_other, 128), :], term_core), around.other)

    def across():
        state["core"].wait_recv()
        mine = lines(half_mine, 128)
        term[mine, :] = term[mine, :] + term_core[...]
        state["across"] = send.copy(lambda: (term.at[lines(quarter_other, 64), :], term_across), around.across)

    def along():
        state["across"].wait_recv()
        mine = lines(quarter_mine, 64)
        term[mine, :] = term[mine, :] + term_across[...]
        state["x"] = [
            send.copy(lambda dx=dx: (term.at[lines(quarter_mine + ((here.x + dx) % 4) * 16, 16), :], term_x.at[dx - 1]), around.ahead[dx - 1])
            for dx in (1, 2, 3)
        ]

    def over_y():
        for made in state["x"]:
            made.wait_recv()
        chunk_sum[0] = term[lines(piece_mine, 16), :] + term_x[0] + term_x[1] + term_x[2]
        state["y"] = [
            send.copy(lambda slot=slot: (chunk_sum.at[0], term_y.at[slot]), around.beside[slot]) for slot in range(3)
        ]

    def over_z():
        for made in state["y"]:
            made.wait_recv()
        chunk_sum[1] = (chunk_sum[0] + term_y[1]) + (term_y[0] + term_y[2])
        state["z"] = [
            send.copy(lambda slot=slot: (chunk_sum.at[1], term_z.at[slot]), around.levels[slot]) for slot in range(3)
        ]

    def whole_x():
        for made in state["z"]:
            made.wait_recv()
        piece = lines(piece_mine, 16)
        grad_weight[piece, :] = (chunk_sum[1] + term_z[0]) + (term_z[1] + term_z[2])
        state["all_x"] = [same(piece_mine, 16, around.ahead[slot]) for slot in range(3)]

    def whole_across():
        for made in state["all_x"]:
            made.wait_recv()
        state["all_across"] = same(quarter_mine, 64, around.across)

    def whole_core():
        state["all_across"].wait_recv()
        state["all_core"] = same(half_mine, 128, around.other)

    def end():
        state["all_core"].wait_recv()

    return [core, across, along, over_y, over_z, whole_x, whole_across, whole_core, end]


def layer_kernel(plan, features, weight, cotangent, tiles, output, grad_weight, grad_input, *rest):
    (
        sources, backs, parts, parts_back, held, prefix, running,
        from_left, from_right, full_left, full_right, merged_right, merged_left,
        level_send, level_recv, total, aggregated,
        core_recv, merged, x_from_left, x_from_right, x_full_left, x_full_right,
        x_merged_right, x_merged_left, x_level_send, x_level_recv, result,
        term, term_core, term_across, term_x, term_y, term_z, chunk_sum,
        tile_sem, send_sems, recv_sems,
    ) = rest
    slots = held.shape[0]
    prefix[slots] = jnp.zeros((TILE, HALF), BF16)
    load = pltpu.make_async_copy(tiles, held, tile_sem)
    load.start()
    around = Around(Place())
    here = around.here
    greet(around.everyone())
    send = Sender(send_sems, recv_sems)
    columns = [pl.ds(half * HALF, HALF) for half in range(2)]

    def product(line, transposed, half, source, placed, services):
        contract = 0 if transposed else 1
        running[...] = jnp.zeros_like(running)

        def group(number, carry):
            for at, steps in services:
                @pl.when(number == at)
                def _():
                    for step in steps:
                        step()

            for step in range(GROUP):
                slot = number * GROUP + step
                block = source[plan[line + 1, slot]]
                fresh = lax.dot_general(
                    held[plan[line, slot]],
                    block,
                    (((contract,), (0,)), ((), ())),
                    preferred_element_type=F32,
                )
                running[...] = fresh + plan[line + 2, slot].astype(F32) * running[...]
                prefix[slot] = running[...].astype(BF16)
            return carry

        lax.fori_loop(0, slots // GROUP, group, 0)

        def place(tile, carry):
            placed[rows_at(tile * TILE, TILE), :] = prefix[plan[line + 3, tile]]
            return carry

        lax.fori_loop(0, TILES, place, 0, unroll=4)

    mine = here.at()[0] * 2
    gathers = []
    for half in range(2):
        for part in range(2):
            sources[half][mine + part] = features[pl.ds(part * TILE, TILE), columns[half]]
        gathers.append(gather_steps(around, send, sources[half]))
    one, two = gathers
    one[0]()
    one[1]()
    two[0]()
    one[2]()
    two[1]()
    one[3]()
    two[2]()
    one[4]()
    one[5]()
    two[3]()
    one[6]()
    load.wait()
    product(0, False, 0, sources[0], parts[0], [(4, two[4:6])])
    two[6]()

    reduces = [
        reduce_steps(
            around, send, parts[half], from_left.at[half], from_right.at[half],
            full_left.at[half], full_right.at[half], merged_right.at[half],
            merged_left.at[half], level_send.at[half], level_recv.at[half],
            total.at[half], aggregated.at[half],
        )
        for half in range(2)
    ]
    one, two = reduces
    one[0]()
    product(0, False, 1, sources[1], parts[1], [(4, one[1:2]), (9, one[2:3])])
    two[0]()
    one[3]()
    two[1]()
    one[4]()
    two[2]()
    one[5]()
    two[3]()
    one[6]()
    two[4]()
    two[5]()
    two[6]()

    gathered = jnp.concatenate([aggregated[0], aggregated[1]], axis=1)
    preact = jnp.dot(gathered, weight[...], preferred_element_type=F32)
    squared = preact * preact
    bent = jnp.tanh(SLOPE * (preact + 0.044715 * (preact * squared)))
    output[...] = (0.5 * preact * (1.0 + bent)).astype(BF16)
    slope = 0.5 * (1.0 + bent) + 0.5 * preact * (1.0 - bent * bent) * (
        SLOPE * (1.0 + 3 * 0.044715 * squared)
    )
    delta = (cotangent[...].astype(F32) * slope).astype(BF16)
    back = lax.dot_general(
        delta, weight[...], (((1,), (1,)), ((), ())), preferred_element_type=F32
    ).astype(BF16)
    mine = here.at()[1] * 2
    spreads = []
    for half in range(2):
        for part in range(2):
            backs[half][mine + part] = back[
                part * TILE : (part + 1) * TILE, half * HALF : (half + 1) * HALF
            ]
        spreads.append(spread_steps(around, send, backs[half]))
    one, two = spreads
    one["begin"]()
    term[...] = lax.dot_general(
        gathered, delta, (((0,), (0,)), ((), ())), preferred_element_type=F32
    )
    weights = weight_steps(
        around, send, term, grad_weight, term_core, term_across, term_x, term_y, term_z, chunk_sum
    )
    weights[0]()
    one["level1"]()
    one["far"]()
    one["level2"]()
    two["begin"]()
    one["relay0"]()
    weights[1]()
    one["relay1"]()
    one["level0"]()
    weights[2]()
    two["level1"]()
    two["far"]()
    one["relay2"]()
    two["level2"]()
    two["relay0"]()
    one["relay3"]()
    weights[3]()
    two["level0"]()
    one["end"]()
    product(
        4, True, 0, backs[0], parts_back[0],
        [(2, [two["relay1"]]), (6, [two["relay2"], weights[4]]), (10, [two["relay3"]])],
    )
    scatters = [
        scatter_steps(
            around, send, parts_back[half], result.at[half], core_recv.at[half],
            merged.at[half], x_from_left.at[half], x_from_right.at[half],
            x_full_left.at[half], x_full_right.at[half], x_merged_right.at[half],
            x_merged_left.at[half], x_level_send.at[half], x_level_recv.at[half],
        )
        for half in range(2)
    ]
    one_x, two_x = scatters
    one_x[0]()
    two["end"]()
    weights[5]()
    product(
        4, True, 1, backs[1], parts_back[1],
        [(2, one_x[1:3]), (6, one_x[3:4] + weights[6:7]), (9, one_x[4:5] + weights[7:8])],
    )
    two_x[0]()
    one_x[5]()
    two_x[1]()
    two_x[2]()
    one_x[6]()
    two_x[3]()
    two_x[4]()
    weights[8]()
    two_x[5]()
    two_x[6]()
    for half in range(2):
        grad_input[:, columns[half]] = result[half]
    send.finish()


def layer(plan, features, weight, cotangent, tiles):
    slots = tiles.shape[0]
    block = (TILE, HALF)
    full = (OWNED, HALF)
    nodes = pltpu.VMEM((NODES, HALF), BF16)
    stacked = pltpu.VMEM((TILES, TILE, HALF), BF16)

    def pair(lead, shape):
        return pltpu.VMEM((2, lead) + shape, BF16)

    return pl.pallas_call(
        layer_kernel,
        out_shape=(
            jax.ShapeDtypeStruct((OWNED, WIDTH), BF16),
            jax.ShapeDtypeStruct((WIDTH, WIDTH), F32),
            jax.ShapeDtypeStruct((OWNED, WIDTH), BF16),
        ),
        in_specs=[SMEM_SPEC, VMEM_SPEC, VMEM_SPEC, VMEM_SPEC, ANY_SPEC],
        out_specs=(VMEM_SPEC,) * 3,
        scratch_shapes=[
            [stacked, stacked],
            [stacked, stacked],
            [nodes, nodes],
            [nodes, nodes],
            pltpu.VMEM((slots, TILE, TILE), BF16),
            pltpu.VMEM((slots + 1,) + block, BF16),
            pltpu.VMEM(block, F32),
            pair(4, block),
            pair(4, block),
            pair(4, full),
            pair(4, full),
            pair(4, block),
            pair(4, block),
            pair(3, full),
            pair(3, full),
            pltpu.VMEM((2,) + full, F32),
            pltpu.VMEM((2,) + full, BF16),
            pair(8, full),
            pair(8, full),
            pair(2, block),
            pair(2, block),
            pair(2, full),
            pair(2, full),
            pair(2, block),
            pair(2, block),
            pltpu.VMEM((2,) + full, BF16),
            pltpu.VMEM((2,) + full, BF16),
            pltpu.VMEM((2,) + full, BF16),
            pltpu.VMEM((WIDTH, WIDTH), F32),
            pltpu.VMEM((128, WIDTH), F32),
            pltpu.VMEM((64, WIDTH), F32),
            pltpu.VMEM((3, 16, WIDTH), F32),
            pltpu.VMEM((3, 16, WIDTH), F32),
            pltpu.VMEM((3, 16, WIDTH), F32),
            pltpu.VMEM((2, 16, WIDTH), F32),
            pltpu.SemaphoreType.DMA,
            pltpu.SemaphoreType.DMA((COPIES,)),
            pltpu.SemaphoreType.DMA((COPIES,)),
        ],
        compiler_params=pltpu.CompilerParams(
            collective_id=0, has_side_effects=True, vmem_limit_bytes=VMEM_LIMIT
        ),
        name="layer",
    )(plan, features, weight, cotangent, tiles)


def shards(features, weight, adjacency, tile_row, tile_col, tile_count, cotangent):
    plan = order_slots(tile_count[0], tile_row[0], tile_col[0])
    return layer(plan, features, weight, cotangent, adjacency[0, 0])


def solution(mesh):
    return jax.shard_map(
        shards,
        mesh=mesh,
        in_specs=(
            P(("row", "col"), None),
            P(),
            P("row", "col", None, None, None),
            P("row", "col", None),
            P("row", "col", None),
            P("row", "col"),
            P(("row", "col"), None),
        ),
        out_specs=(P(("row", "col"), None), P(), P(("row", "col"), None)),
        check_vma=False,
    )
```

time: 763 us -> 116 us (0.15)
  waiting for transfers between devices: 624 us -> 0 us
  Pallas kernels: 0 us -> 109 us
  other arithmetic: 52.1 us -> 0 us
  local copies, waits for them, and re-layouts: 33.1 us -> 4.8 us
  matrix products: 19.4 us -> 0 us
  loops' own time: 16.1 us -> 0 us
  between operations: 13.8 us -> 1.29 us
    reduce_scatter x2 -> x0, waiting for transfers between devices: 280 us -> none  [the longest x1 154 us: shards(): lax.psum_scatter(partial_value, 'col', scatter_dimension=0, tiled=True)]
    psum x1 -> x0, waiting for transfers between devices: 255 us -> none  [shards(): grad_weight = lax.psum(weight_term, ('row', 'col'))]
    pallas_call x0 -> x2, Pallas kernels: none -> 109 us  [the longest x1 107 us: layer(): pl.pallas_call(layer_kernel, out_shape=(jax.ShapeDtypeStruct((OWNED, WIDT...]
    all_gather x2 -> x0, waiting for transfers between devices: 88.8 us -> none  [the longest x1 49.4 us: shards(): back_rows = lax.all_gather(back, 'col', axis=0, tiled=True)]
    scatter-add x4 -> x0, other arithmetic: 39.9 us -> none  [work(): return current.at[placed].add(products * active_group[:, None, None])]
    dot_general x7 -> x0, matrix products: 19.4 us -> none  [the longest x2 7.89 us: work(): jnp.einsum('kab,kaf->kbf', tile_group, blocks[row_group], preferred_eleme...]
    another operation x14 -> x0, loops' own time: 16.1 us -> none  [the longest x2 15.8 us: aggregate(): running, _ = lax.scan(accumulate, initial, packed)]
    convert_element_type x13 -> x0, other arithmetic: 9.44 us -> none  [the longest x12 7.82 us: aggregate(): active = (jnp.arange(slots) < live_count).astype(jnp.float32)]
  transfers between devices with their start and end apart: 5 -> 0, of which waited for: 5 -> 0; matrix products, arithmetic and copies ran while one was open for 2% -> 0% of each run, Pallas kernels for 0% -> 0%
where the time goes in v2:
time: 116 us; the launch traced here: 115 us
  Pallas kernels  109 us (94%)
  local copies, waits for them, and re-layouts  4.8 us (4%)
  between operations  1.29 us (1%)
    pallas_call x1, Pallas kernels, layer(): pl.pallas_call(layer_kernel, out_shape=(jax.ShapeDtypeStruct((OWNED, WIDT...  107 us
    unnamed x3, local copies, waits for them, and re-layouts  4.8 us

profile of v2, /device:TPU:1, one launch (start us, length us, event | category | flops | bytes accessed | tf_op | source)
XLA Modules:
  0.0 115.4 jit_solution(17169477188148495866)
XLA Ops:
  1.3 2.0 %order_slots.1.plan = s32[8,192]{1,0:T(8,128)} custom-call(s32[1]{0:T(128)} %bitcast.4.count_ref, s32[1,192]{1,0:T(1,128)} %bitcast.6, s32[1,192]{1,0:T(1,128)} %bitcast.7), custom_call_target="tpu_custom_call" | custom-call | tf_op jit(solution)/shard_map/order_slots/pallas_call | solution.py:73
  3.3 107.3 %layer.1 = (bf16[256,256]{1,0:T(8,128)(2,1)}, f32[256,256]{1,0:T(8,128)}, bf16[256,256]{1,0:T(8,128)(2,1)}) custom-call(s32[8,192]{1,0:T(8,128)} %order_slots.1.plan, bf16[256,256]{1,0:T(8,128)(2,1)} %features.1, bf16[256,256]{1,0:T(8,128)(2,1)} %weight.1, bf16[256,256]{1,0:T(8,128)(2,1)} %cotangent.1, bf16[192,128,128]{2,1,0:T(8,128)(2,1)} %bitcast.5), custom_call_target="tpu_custom_call" | custom-call | tf_op jit(solution)/shard_map/layer/pallas_call | solution.py:697
  110.6 1.6 %copy.14 = bf16[256,256]{1,0:T(8,128)(2,1)} copy(bf16[256,256]{1,0:T(8,128)(2,1)} %get-tuple-element.6) | data formatting | bytes 262144
  112.2 1.7 %copy.15 = f32[256,256]{1,0:T(8,128)} copy(f32[256,256]{1,0:T(8,128)} %get-tuple-element.7) | data formatting | bytes 524288
  113.9 1.6 %copy.16 = bf16[256,256]{1,0:T(8,128)(2,1)} copy(bf16[256,256]{1,0:T(8,128)(2,1)} %get-tuple-element.8) | data formatting | bytes 262144

commit v3 on v0

v3 whole, which is shorter than its diff:
```python
import functools
import math

import jax
import jax.numpy as jnp
from jax import lax
from jax.experimental import pallas as pl
from jax.experimental.pallas import tpu as pltpu
from jax.sharding import PartitionSpec as P

MESH = pl.DeviceIdType.MESH
BF16 = jnp.bfloat16
F32 = jnp.float32
TILE = 128
OWNED = 256
WIDTH = 256
HALF = 128
NODES = 4096
TILES = NODES // TILE
GROUP = 32
COPIES = 128
LOADS = 4
GATHER_BEGIN = ("g0.own", "g1.own",)
GATHER_FIRST = ("g0.core0", "g0.core1", "g0.core3", "g0.core2", "g0.end",)
GATHER_DURING = ((2, ("g1.core0", "g1.core1",)), (4, ("g1.core3", "g1.core2",)))
GATHER_LAST = ("g1.end",)
REDUCE_FIRST = ("r0.first0", "r0.first1", "r0.plain",)
REDUCE_DURING = ((5, ("r0.merge",)),)
REDUCE_LAST = ("r0.late", "r0.last", "r1.first0", "r1.first1", "r1.plain", "r0.sum2", "r0.sum3", "r0.sum1", "r0.sum0", "r1.merge", "r1.late", "r1.last", "r0.end", "r1.sum2", "r1.sum3", "r1.sum1", "r1.sum0", "r1.end",)
SPREAD_BEGIN = ("s0.begin", "s0.far", "s1.begin", "s1.far",)
SPREAD_FIRST = ("w.weight0", "s0.relay0", "s1.relay0", "s0.level1", "s0.level2", "s0.level0", "s0.relay3", "s0.relay1", "w.weight1", "s1.level1", "s1.level2", "s1.level0", "w.weight2", "s0.end",)
SPREAD_DURING = ((1, ("s1.relay3",)), (3, ("s1.relay1", "w.weight3",)))
SPREAD_LAST = ("c0.cores", "s1.end", "w.weight4",)
SCATTER_DURING = ((2, ("c0.chips0",)), (3, ("c0.chips1", "w.weight5",)), (5, ("w.weight6",)))
SCATTER_LAST = ("c1.cores", "w.weight7", "c1.chips0", "c1.chips1", "w.weight8", "c0.end", "c1.end",)
VMEM_LIMIT = 58 * 1024 * 1024
SLOPE = math.sqrt(2 / math.pi)

VMEM_SPEC = pl.BlockSpec(memory_space=pltpu.VMEM)
SMEM_SPEC = pl.BlockSpec(memory_space=pltpu.SMEM)
ANY_SPEC = pl.BlockSpec(memory_space=pl.ANY)
LOW = pl.ds(0, TILE)
HIGH = pl.ds(TILE, TILE)


def gather_place(tile):
    return (tile & 2) * 8 + (tile >> 3) * 4 + ((tile >> 2) & 1) * 2 + (tile & 1)


def scatter_place(tile):
    return (tile & 2) * 8 + ((tile >> 2) & 1) * 8 + (tile >> 3) * 2 + (tile & 1)


def arrange(placed, taken, live):
    slots = placed.shape[1]
    lane = lax.broadcasted_iota(jnp.int32, (slots, slots), 1)
    line = lax.broadcasted_iota(jnp.int32, (slots, slots), 0)

    def turned(flat):
        return jnp.sum(jnp.where(lane == line, flat, 0), axis=1, keepdims=True)

    lane_row = lax.broadcasted_iota(jnp.int32, (1, slots), 1)
    tagged = jnp.where(lane_row < live, placed, TILES)
    key = tagged * 256 + lane_row
    rank = jnp.sum(jnp.where(key < turned(key), 1, 0), axis=1, keepdims=True)
    tag_line = turned(tagged)
    taken_line = turned(taken)
    chosen = rank == lane

    def pick(column):
        return jnp.sum(jnp.where(chosen, column, 0), axis=0, keepdims=True)

    order = pick(line)
    source = pick(taken_line)
    tag = pick(tag_line + 1)
    before = jnp.sum(jnp.where(rank + 1 == lane, tag_line + 1, 0), axis=0, keepdims=True)
    keep = jnp.where(tag == before, 1, 0)
    up_to = jnp.sum(jnp.where(tag_line <= lane, 1, 0), axis=0, keepdims=True)
    here = jnp.sum(jnp.where(tag_line == lane, 1, 0), axis=0, keepdims=True)
    last = jnp.where(here > 0, up_to - 1, slots)
    return (order, source, keep, last)


class Place:
    def __init__(self):
        row = lax.axis_index("row")
        col = lax.axis_index("col")
        four, two = jnp.int32(4), jnp.int32(2)
        self.x = lax.div(row, four)
        self.zl = lax.rem(lax.div(row, two), two)
        self.core = lax.rem(row, two)
        self.y = lax.div(col, four)
        self.zh = lax.rem(col, four)
        xs = [lax.rem(self.x + step, four) * 4 for step in range(4)]
        zls = [self.zl * 2, 2 - self.zl * 2]
        cores = [self.core, 1 - self.core]
        ys = [lax.rem(self.y + step, four) * 4 for step in range(4)]
        zhs = [lax.rem(self.zh + step, four) for step in range(4)]
        self.rows = [[[x + zl + core for core in cores] for zl in zls] for x in xs]
        self.gather_tiles = [[cores[0] * 16 + x + zl for zl in zls] for x in xs]
        self.gather_pairs = [cores[0] * 16 + x for x in xs]
        self.scatter_groups = [[core * 16 + zl * 4 for zl in zls] for core in cores]
        self.scatter_spots = [lax.rem(self.x + step, four) * 2 for step in range(4)]
        self.cols = [[y + zh for zh in zhs] for y in ys]

    def at(self, dx=0, dzl=0, dcore=0, dy=0, dzh=0):
        return (self.rows[dx % 4][dzl % 2][dcore % 2], self.cols[dy % 4][dzh % 4])


class Copy:
    def __init__(self, describe):
        self.describe = describe

    def wait_recv(self):
        self.describe().wait_recv()

    def wait_send(self):
        self.describe().wait_send()


class Sender:
    def __init__(self, send_sems, recv_sems):
        self.send_sems = send_sems
        self.recv_sems = recv_sems
        self.started = []

    def copy(self, ends, device):
        used = len(self.started)

        def describe():
            src, dst = ends()
            return pltpu.make_async_remote_copy(
                src_ref=src,
                dst_ref=dst,
                send_sem=self.send_sems.at[used],
                recv_sem=self.recv_sems.at[used],
                device_id=device,
                device_id_type=MESH,
            )

        describe().start()
        made = Copy(describe)
        self.started.append(made)
        return made

    def finish(self):
        for made in self.started:
            made.wait_send()


def rows_at(start, size):
    return pl.ds(pl.multiple_of(start, TILE), size)


class Around:
    def __init__(self, here):
        self.here = here
        self.other = here.at(dcore=1)
        self.across = here.at(dzl=1)
        self.ahead = [here.at(dx=step) for step in (1, 2, 3)]
        self.beside = [here.at(dy=step) for step in (1, 2, 3)]
        self.levels = [here.at(dzh=step) for step in (2, 1, 3)]

    def everyone(self):
        here = self.here
        group = [here.at(dx=dx, dzl=dzl) for dx in range(4) for dzl in range(2) if dx or dzl]
        return [self.other] + group + self.beside + self.levels


def gather_steps(around, send, gathered):
    here = around.here
    made = {}

    def move(start, size, device):
        def ends():
            block = gathered.at[pl.ds(start, size)]
            return block, block

        return send.copy(ends, device)

    def own():
        for dx, dzl in ((0, 1), (1, 0), (3, 0), (1, 1), (3, 1), (2, 0), (2, 1)):
            made[dx, dzl] = move(here.gather_tiles[0][0], 2, here.at(dx=dx, dzl=dzl))

    def to_core(dx):
        for dzl in range(2):
            if dx or dzl:
                made[-dx % 4, dzl].wait_recv()
        made[dx] = move(here.gather_pairs[dx], 4, around.other)

    def end():
        for dx in range(4):
            made[dx].wait_recv()

    steps = {"own": own, "end": end}
    for dx in range(4):
        steps[f"core{dx}"] = functools.partial(to_core, dx)
    return steps


def reduce_steps(
    around, send, parts, from_left, from_right, full_left, full_right, merged,
    level_send, level_recv, total, result,
):
    here = around.here
    right, left = around.beside[0], around.beside[2]
    by_right, by_left = (2, 1), (3, 0)
    level_of = {2: 0, 1: 1, 3: 2}
    firsts, lefts, rights, levels = {}, {}, {}, {}

    def where(dy, dzh):
        return rows_at(here.at(dy=dy, dzh=dzh)[1] * OWNED, OWNED)

    def first(number):
        dzh = by_right[number]
        firsts[dzh] = send.copy(
            lambda: (parts.at[where(2, by_right[number]), :], from_left.at[number]), right
        )
        dzh = by_left[number]
        firsts[dzh] = send.copy(
            lambda: (parts.at[where(2, by_left[number]), :], from_right.at[number]), left
        )

    def to_right(dzh, source):
        rights[dzh] = send.copy(lambda: (source(), full_left.at[dzh]), right)

    def to_left(dzh, source):
        lefts[dzh] = send.copy(lambda: (source(), full_right.at[dzh]), left)

    def plain():
        to_right(3, lambda: parts.at[where(1, 3), :])
        to_left(2, lambda: parts.at[where(-1, 2), :])

    def merge_right(number):
        dzh = by_right[number]
        firsts[dzh].wait_recv()
        merged[dzh] = (
            parts[where(1, dzh), :].astype(F32) + from_left[number].astype(F32)
        ).astype(BF16)
        to_right(dzh, lambda: merged.at[dzh])

    def merge_left(number):
        dzh = by_left[number]
        firsts[dzh].wait_recv()
        merged[dzh] = (
            parts[where(-1, dzh), :].astype(F32) + from_right[number].astype(F32)
        ).astype(BF16)
        to_left(dzh, lambda: merged.at[dzh])

    def merge():
        merge_right(0)
        merge_left(0)

    def late():
        to_left(1, lambda: parts.at[where(-1, 1), :])
        merge_right(1)

    def last():
        to_right(0, lambda: parts.at[where(1, 0), :])
        merge_left(1)

    def complete(dzh):
        rights[dzh].wait_recv()
        lefts[dzh].wait_recv()
        summed = (
            parts[where(0, dzh), :].astype(F32)
            + full_left[dzh].astype(F32)
            + full_right[dzh].astype(F32)
        )
        if dzh:
            slot = level_of[dzh]
            level_send[slot] = summed.astype(BF16)
            levels[slot] = send.copy(
                lambda: (level_send.at[slot], level_recv.at[slot]), around.levels[slot]
            )
        else:
            total[...] = summed

    def end():
        for slot in range(3):
            levels[slot].wait_recv()
        result[...] = (
            total[...]
            + level_recv[0].astype(F32)
            + level_recv[1].astype(F32)
            + level_recv[2].astype(F32)
        ).astype(BF16)

    steps = {"plain": plain, "merge": merge, "late": late, "last": last, "end": end}
    for number in range(2):
        steps[f"first{number}"] = functools.partial(first, number)
    for dzh in range(4):
        steps[f"sum{dzh}"] = functools.partial(complete, dzh)
    return steps


def spread_steps(around, send, gathered):
    here = around.here
    right, left = around.beside[0], around.beside[2]
    up, ring_right, ring_left, relays = {}, {}, {}, []
    came = {0: 2, 1: 3, 2: 1}

    def move(dy, dzh, device):
        def ends():
            block = gathered.at[pl.ds(here.at(dy=dy, dzh=dzh)[1] * 2, 2)]
            return block, block

        return send.copy(ends, device)

    def ring(dzh):
        ring_right[dzh] = move(0, dzh, right)
        ring_left[dzh] = move(0, dzh, left)

    def begin():
        up[1] = move(0, 0, around.levels[1])
        up[2] = move(0, 0, around.levels[2])
        ring(0)

    def far():
        up[0] = move(0, 0, around.levels[0])

    def level(slot):
        up[slot].wait_recv()
        ring(came[slot])
        if slot == 0:
            relays.append(move(0, 2, around.beside[1]))

    def relay(dzh):
        if dzh == 0:
            ring_right[dzh].wait_recv()
            relays.append(move(-1, dzh, right))
        else:
            ring_left[dzh].wait_recv()
            relays.append(move(1, dzh, left))

    def end():
        for dzh in (0, 2):
            ring_left[dzh].wait_recv()
        for dzh in (1, 2, 3):
            ring_right[dzh].wait_recv()
        for made in relays:
            made.wait_recv()

    steps = {"begin": begin, "far": far, "end": end}
    for slot in range(3):
        steps[f"level{slot}"] = functools.partial(level, slot)
    for dzh in (0, 1, 3):
        steps[f"relay{dzh}"] = functools.partial(relay, dzh)
    return steps


def scatter_steps(around, send, parts, out, core_recv, sent, received):
    here = around.here
    cores, made = [], {}

    def begin():
        for step in range(2):
            start = here.scatter_groups[1][1 - step] * TILE
            cores.append(
                send.copy(
                    lambda start=start, step=step: (
                        parts.at[rows_at(start, 4 * OWNED), :], core_recv.at[step]
                    ),
                    around.other,
                )
            )

    def collect(dx, step):
        spot = here.scatter_spots[dx]
        mine = rows_at((here.scatter_groups[0][1 - step] + spot) * TILE, OWNED)
        theirs = rows_at(spot * TILE, OWNED)
        return parts[mine, :].astype(F32) + core_recv[step, theirs, :].astype(F32)

    def chips(step):
        cores[step].wait_recv()
        for dx in (2, 1, 3, 0):
            slot = 4 * step + dx
            if slot != 4:
                sent[slot] = collect(dx, step).astype(BF16)
                made[slot] = send.copy(
                    lambda slot=slot: (sent.at[slot], received.at[slot]),
                    here.at(dx=dx, dzl=1 - step),
                )

    def end():
        summed = collect(0, 1)
        for slot in made:
            made[slot].wait_recv()
        for slot in made:
            summed = summed + received[slot].astype(F32)
        out[...] = summed.astype(BF16)

    return {
        "cores": begin,
        "chips0": functools.partial(chips, 0),
        "chips1": functools.partial(chips, 1),
        "end": end,
    }


def weight_steps(
    around, send, term, grad_weight, term_core, term_across, term_x, term_y, term_z, chunk_sum
):
    here = around.here
    half_mine = here.core * 128
    half_other = 128 - half_mine
    quarter_mine = half_mine + here.zl * 64
    quarter_other = half_mine + 64 - here.zl * 64
    piece_mine = quarter_mine + here.x * 16
    state = {}

    def lines(start, size):
        return pl.ds(pl.multiple_of(start, size), size)

    def same(start, size, device):
        def ends():
            block = grad_weight.at[lines(start, size), :]
            return block, block

        return send.copy(ends, device)

    def core():
        state["core"] = send.copy(lambda: (term.at[lines(half_other, 128), :], term_core), around.other)

    def across():
        state["core"].wait_recv()
        mine = lines(half_mine, 128)
        term[mine, :] = term[mine, :] + term_core[...]
        state["across"] = send.copy(lambda: (term.at[lines(quarter_other, 64), :], term_across), around.across)

    def along():
        state["across"].wait_recv()
        mine = lines(quarter_mine, 64)
        term[mine, :] = term[mine, :] + term_across[...]
        state["x"] = [
            send.copy(lambda dx=dx: (term.at[lines(quarter_mine + lax.rem(here.x + dx, jnp.int32(4)) * 16, 16), :], term_x.at[dx - 1]), around.ahead[dx - 1])
            for dx in (1, 2, 3)
        ]

    def over_y():
        for made in state["x"]:
            made.wait_recv()
        chunk_sum[0] = term[lines(piece_mine, 16), :] + term_x[0] + term_x[1] + term_x[2]
        state["y"] = [
            send.copy(lambda slot=slot: (chunk_sum.at[0], term_y.at[slot]), around.beside[slot]) for slot in range(3)
        ]

    def over_z():
        for made in state["y"]:
            made.wait_recv()
        chunk_sum[1] = (chunk_sum[0] + term_y[1]) + (term_y[0] + term_y[2])
        state["z"] = [
            send.copy(lambda slot=slot: (chunk_sum.at[1], term_z.at[slot]), around.levels[slot]) for slot in range(3)
        ]

    def whole_x():
        for made in state["z"]:
            made.wait_recv()
        piece = lines(piece_mine, 16)
        grad_weight[piece, :] = (chunk_sum[1] + term_z[0]) + (term_z[1] + term_z[2])
        state["all_x"] = [same(piece_mine, 16, around.ahead[slot]) for slot in range(3)]

    def whole_across():
        for made in state["all_x"]:
            made.wait_recv()
        state["all_across"] = same(quarter_mine, 64, around.across)

    def whole_core():
        state["all_across"].wait_recv()
        state["all_core"] = same(half_mine, 128, around.other)

    def end():
        state["all_core"].wait_recv()

    found = (core, across, along, over_y, over_z, whole_x, whole_across, whole_core, end)
    return {f"weight{number}": step for number, step in enumerate(found)}


def run(streams, names):
    for name in names:
        stream, step = name.split(".")
        streams[stream][step]()


def layer_kernel(
    count, tile_row, tile_col, features, weight, cotangent, tiles,
    output, grad_weight, grad_input, *rest
):
    (
        sources, backs, parts, parts_back, held, prefix, running,
        reduce_scratch, scatter_scratch, results, grads,
        term, term_core, term_across, term_x, term_y, term_z, chunk_sum,
        plan_lines, plan, plan_sem, tile_sem, send_sems, recv_sems,
    ) = rest
    slots = held.shape[0]
    share = slots // LOADS
    loads = [
        pltpu.make_async_copy(
            tiles.at[pl.ds(number * share, share)],
            held.at[pl.ds(number * share, share)],
            tile_sem.at[number],
        )
        for number in range(LOADS)
    ]
    for load in loads:
        load.start()
    around = Around(Place())
    here = around.here
    barrier = pltpu.get_barrier_semaphore()
    devices = around.everyone()
    for device in devices:
        pl.semaphore_signal(barrier, inc=1, device_id=device, device_id_type=MESH)
    pl.semaphore_wait(barrier, len(devices))
    send = Sender(send_sems, recv_sems)
    columns = [pl.ds(half * HALF, HALF) for half in range(2)]

    def product(line, transposed, half, source, placed, services):
        contract = 0 if transposed else 1
        running[...] = jnp.zeros_like(running)

        def group(number, carry):
            for at, names in services:
                @pl.when(number == at)
                def _():
                    run(streams, names)

            for step in range(GROUP):
                slot = number * GROUP + step
                block = source[plan[line + 1, slot]]
                fresh = lax.dot_general(
                    held[plan[line, slot]],
                    block,
                    (((contract,), (0,)), ((), ())),
                    preferred_element_type=F32,
                )
                running[...] = fresh + plan[line + 2, slot].astype(F32) * running[...]
                prefix[slot] = running[...].astype(BF16)
            return carry

        lax.fori_loop(0, slots // GROUP, group, 0)

        def place(tile, carry):
            placed[rows_at(tile * TILE, TILE), :] = prefix[plan[line + 3, tile]]
            return carry

        lax.fori_loop(0, TILES, place, 0, unroll=4)

    streams = {}
    mine = here.gather_tiles[0][0]
    for half in range(2):
        for part in range(2):
            sources[half][mine + part] = features[pl.ds(part * TILE, TILE), columns[half]]
        streams[f"g{half}"] = gather_steps(around, send, sources[half])
        streams[f"r{half}"] = reduce_steps(
            around, send, parts[half], *[ref.at[half] for ref in reduce_scratch], results.at[half]
        )
        streams[f"s{half}"] = spread_steps(around, send, backs[half])
        streams[f"c{half}"] = scatter_steps(
            around, send, parts_back[half], grads.at[half],
            *[ref.at[half] for ref in scatter_scratch],
        )
    streams["w"] = weight_steps(
        around, send, term, grad_weight, term_core, term_across, term_x, term_y, term_z, chunk_sum
    )
    run(streams, GATHER_BEGIN)
    prefix[slots] = jnp.zeros((TILE, HALF), BF16)
    live = count[0]
    rows = tile_row[...]
    cols = tile_col[...]
    found = arrange(rows, gather_place(cols), live) + arrange(scatter_place(cols), rows, live)
    for line, value in enumerate(found):
        plan_lines[line : line + 1, :] = value
    load_plan = pltpu.make_async_copy(plan_lines, plan, plan_sem)
    load_plan.start()
    run(streams, GATHER_FIRST)
    for load in loads:
        load.wait()
    load_plan.wait()
    product(0, False, 0, sources[0], parts[0], GATHER_DURING)
    run(streams, GATHER_LAST)
    run(streams, REDUCE_FIRST)
    product(0, False, 1, sources[1], parts[1], REDUCE_DURING)
    run(streams, REDUCE_LAST)

    gathered = jnp.concatenate([results[0], results[1]], axis=1)
    preact = jnp.dot(gathered, weight[...], preferred_element_type=F32)
    squared = preact * preact
    bent = jnp.tanh(SLOPE * (preact + 0.044715 * (preact * squared)))
    slope = 0.5 * (1.0 + bent) + 0.5 * preact * (1.0 - bent * bent) * (
        SLOPE * (1.0 + 3 * 0.044715 * squared)
    )
    delta = (cotangent[...].astype(F32) * slope).astype(BF16)
    back = lax.dot_general(
        delta, weight[...], (((1,), (1,)), ((), ())), preferred_element_type=F32
    ).astype(BF16)
    mine = here.at()[1] * 2
    for half in range(2):
        for part in range(2):
            backs[half][mine + part] = back[
                part * TILE : (part + 1) * TILE, half * HALF : (half + 1) * HALF
            ]
    run(streams, SPREAD_BEGIN)
    output[...] = (0.5 * preact * (1.0 + bent)).astype(BF16)
    term[...] = lax.dot_general(
        gathered, delta, (((0,), (0,)), ((), ())), preferred_element_type=F32
    )
    run(streams, SPREAD_FIRST)
    product(4, True, 0, backs[0], parts_back[0], SPREAD_DURING)
    run(streams, SPREAD_LAST)
    product(4, True, 1, backs[1], parts_back[1], SCATTER_DURING)
    run(streams, SCATTER_LAST)
    for half in range(2):
        grad_input[:, columns[half]] = grads[half]
    send.finish()


def layer(count, tile_row, tile_col, features, weight, cotangent, tiles):
    slots = tiles.shape[0]
    block = (TILE, HALF)
    full = (OWNED, HALF)
    nodes = pltpu.VMEM((NODES, HALF), BF16)
    stacked = pltpu.VMEM((TILES, TILE, HALF), BF16)

    single = pltpu.VMEM((2,) + full, BF16)

    def pair(lead):
        return pltpu.VMEM((2, lead) + full, BF16)

    return pl.pallas_call(
        layer_kernel,
        out_shape=(
            jax.ShapeDtypeStruct((OWNED, WIDTH), BF16),
            jax.ShapeDtypeStruct((WIDTH, WIDTH), F32),
            jax.ShapeDtypeStruct((OWNED, WIDTH), BF16),
        ),
        in_specs=[SMEM_SPEC] + [VMEM_SPEC] * 5 + [ANY_SPEC],
        out_specs=(VMEM_SPEC,) * 3,
        scratch_shapes=[
            [stacked, stacked],
            [stacked, stacked],
            [nodes, nodes],
            [nodes, nodes],
            pltpu.VMEM((slots, TILE, TILE), BF16),
            pltpu.VMEM((slots + 1,) + block, BF16),
            pltpu.VMEM(block, F32),
            [pair(lead) for lead in (2, 2, 4, 4, 4, 3, 3)] + [pltpu.VMEM((2,) + full, F32)],
            [pltpu.VMEM((2, 2, 4 * OWNED, HALF), BF16), pair(8), pair(8)],
            single,
            single,
            pltpu.VMEM((WIDTH, WIDTH), F32),
            pltpu.VMEM((128, WIDTH), F32),
            pltpu.VMEM((64, WIDTH), F32),
            pltpu.VMEM((3, 16, WIDTH), F32),
            pltpu.VMEM((3, 16, WIDTH), F32),
            pltpu.VMEM((3, 16, WIDTH), F32),
            pltpu.VMEM((2, 16, WIDTH), F32),
            pltpu.VMEM((8, slots), jnp.int32),
            pltpu.SMEM((8, slots), jnp.int32),
            pltpu.SemaphoreType.DMA,
            pltpu.SemaphoreType.DMA((LOADS,)),
            pltpu.SemaphoreType.DMA((COPIES,)),
            pltpu.SemaphoreType.DMA((COPIES,)),
        ],
        compiler_params=pltpu.CompilerParams(
            collective_id=0, has_side_effects=True, vmem_limit_bytes=VMEM_LIMIT
        ),
        name="layer",
    )(count, tile_row, tile_col, features, weight, cotangent, tiles)


def hand_on_kernel(*refs):
    for number in range(3):
        refs[number + 3][...] = refs[number][...]


def hand_on(*arrays):
    return pl.pallas_call(
        hand_on_kernel,
        out_shape=tuple(jax.ShapeDtypeStruct(array.shape, array.dtype) for array in arrays),
        in_specs=[VMEM_SPEC] * 3,
        out_specs=(VMEM_SPEC,) * 3,
        name="hand_on",
    )(*arrays)


def shards(features, weight, adjacency, tile_row, tile_col, tile_count, cotangent):
    return hand_on(
        *layer(
            tile_count[0], tile_row[0], tile_col[0], features, weight, cotangent, adjacency[0, 0]
        )
    )


def solution(mesh):
    return jax.shard_map(
        shards,
        mesh=mesh,
        in_specs=(
            P(("row", "col"), None),
            P(),
            P("row", "col", None, None, None),
            P("row", "col", None),
            P("row", "col", None),
            P("row", "col"),
            P(("row", "col"), None),
        ),
        out_specs=(P(("row", "col"), None), P(), P(("row", "col"), None)),
        check_vma=False,
    )
```

time: 763 us -> 107 us (0.14)
  waiting for transfers between devices: 624 us -> 0 us
  Pallas kernels: 0 us -> 105 us
  other arithmetic: 52.1 us -> 0 us
  local copies, waits for them, and re-layouts: 33.1 us -> 0 us
  matrix products: 19.4 us -> 0 us
  loops' own time: 16.1 us -> 0 us
  between operations: 13.8 us -> 1.29 us
    reduce_scatter x2 -> x0, waiting for transfers between devices: 280 us -> none  [the longest x1 154 us: shards(): lax.psum_scatter(partial_value, 'col', scatter_dimension=0, tiled=True)]
    psum x1 -> x0, waiting for transfers between devices: 255 us -> none  [shards(): grad_weight = lax.psum(weight_term, ('row', 'col'))]
    pallas_call x0 -> x2, Pallas kernels: none -> 105 us  [the longest x1 103 us: layer(): pl.pallas_call(layer_kernel, out_shape=(jax.ShapeDtypeStruct((OWNED, WIDT...]
    all_gather x2 -> x0, waiting for transfers between devices: 88.8 us -> none  [the longest x1 49.4 us: shards(): back_rows = lax.all_gather(back, 'col', axis=0, tiled=True)]
    scatter-add x4 -> x0, other arithmetic: 39.9 us -> none  [work(): return current.at[placed].add(products * active_group[:, None, None])]
    dot_general x7 -> x0, matrix products: 19.4 us -> none  [the longest x2 7.89 us: work(): jnp.einsum('kab,kaf->kbf', tile_group, blocks[row_group], preferred_eleme...]
    another operation x14 -> x0, loops' own time: 16.1 us -> none  [the longest x2 15.8 us: aggregate(): running, _ = lax.scan(accumulate, initial, packed)]
    unnamed x9 -> x0, local copies, waits for them, and re-layouts: 11.7 us -> none
  transfers between devices with their start and end apart: 5 -> 0, of which waited for: 5 -> 0; matrix products, arithmetic and copies ran while one was open for 2% -> 0% of each run, Pallas kernels for 0% -> 0%
where the time goes in v3:
time: 107 us
  Pallas kernels  105 us (98%)
  between operations  1.29 us (1%)
    pallas_call x1, Pallas kernels, layer(): pl.pallas_call(layer_kernel, out_shape=(jax.ShapeDtypeStruct((OWNED, WIDT...  103 us

profile of v3, /device:TPU:1, one launch (start us, length us, event | category | flops | bytes accessed | tf_op | source)
XLA Modules:
  0.0 106.5 jit_solution(1516177408143516504)
XLA Ops:
  1.3 103.4 %layer.1 = (bf16[256,256]{1,0:T(8,128)(2,1)}, f32[256,256]{1,0:T(8,128)}, bf16[256,256]{1,0:T(8,128)(2,1)}) custom-call(s32[1]{0:T(128)} %bitcast.4.count, s32[1,192]{1,0:T(1,128)} %bitcast.6, s32[1,192]{1,0:T(1,128)} %bitcast.7, bf16[256,256]{1,0:T(8,128)(2,1)} %features.1, bf16[256,256]{1,0:T(8,128)(2,1)} %weight.1, bf16[256,256]{1,0:T(8,128)(2,1)} %cotangent.1, ...), custom_call_target="tpu_custom_call" | custom-call | tf_op jit(solution)/shard_map/layer/pallas_call | solution.py:629
  104.7 1.8 %hand_on.1 = (bf16[256,256]{1,0:T(8,128)(2,1)}, f32[256,256]{1,0:T(8,128)}, bf16[256,256]{1,0:T(8,128)(2,1)}) custom-call(bf16[256,256]{1,0:T(8,128)(2,1)} %get-tuple-element.6.refs_0_, f32[256,256]{1,0:T(8,128)} %get-tuple-element.7.refs_1_, bf16[256,256]{1,0:T(8,128)(2,1)} %get-tuple-element.8.refs_2_), custom_call_target="tpu_custom_call" | custom-call | tf_op jit(solution)/shard_map/hand_on/pallas_call | solution.py:677

commit v4 on v3

--- a/solution.py
+++ b/solution.py
@@ -17,21 +17,22 @@
 HALF = 128
 NODES = 4096
 TILES = NODES // TILE
-GROUP = 32
+GROUP = 64
 COPIES = 128
+BY_RIGHT = ((0,), (0, 3))
 LOADS = 4
 GATHER_BEGIN = ("g0.own", "g1.own",)
 GATHER_FIRST = ("g0.core0", "g0.core1", "g0.core3", "g0.core2", "g0.end",)
-GATHER_DURING = ((2, ("g1.core0", "g1.core1",)), (4, ("g1.core3", "g1.core2",)))
+GATHER_DURING = ((1,("g1.core0","g1.core1","g1.core3","g1.core2")),)
 GATHER_LAST = ("g1.end",)
 REDUCE_FIRST = ("r0.first0", "r0.first1", "r0.plain",)
-REDUCE_DURING = ((5, ("r0.merge",)),)
+REDUCE_DURING = ((2,("r0.merge",)),)
 REDUCE_LAST = ("r0.late", "r0.last", "r1.first0", "r1.first1", "r1.plain", "r0.sum2", "r0.sum3", "r0.sum1", "r0.sum0", "r1.merge", "r1.late", "r1.last", "r0.end", "r1.sum2", "r1.sum3", "r1.sum1", "r1.sum0", "r1.end",)
 SPREAD_BEGIN = ("s0.begin", "s0.far", "s1.begin", "s1.far",)
 SPREAD_FIRST = ("w.weight0", "s0.relay0", "s1.relay0", "s0.level1", "s0.level2", "s0.level0", "s0.relay3", "s0.relay1", "w.weight1", "s1.level1", "s1.level2", "s1.level0", "w.weight2", "s0.end",)
-SPREAD_DURING = ((1, ("s1.relay3",)), (3, ("s1.relay1", "w.weight3",)))
+SPREAD_DURING = ((1,("s1.relay3",)),(2,("s1.relay1","w.weight3")))
 SPREAD_LAST = ("c0.cores", "s1.end", "w.weight4",)
-SCATTER_DURING = ((2, ("c0.chips0",)), (3, ("c0.chips1", "w.weight5",)), (5, ("w.weight6",)))
+SCATTER_DURING = ((1,("c0.chips0","c0.chips1","w.weight5")),(2,("w.weight6",)))
 SCATTER_LAST = ("c1.cores", "w.weight7", "c1.chips0", "c1.chips1", "w.weight8", "c0.end", "c1.end",)
 VMEM_LIMIT = 58 * 1024 * 1024
 SLOPE = math.sqrt(2 / math.pi)
@@ -294,7 +295,7 @@
     return steps
 
 
-def spread_steps(around, send, gathered):
+def spread_steps(around, send, gathered, by_right):
     here = around.here
     right, left = around.beside[0], around.beside[2]
     up, ring_right, ring_left, relays = {}, {}, {}, []
@@ -326,7 +327,7 @@
             relays.append(move(0, 2, around.beside[1]))
 
     def relay(dzh):
-        if dzh == 0:
+        if dzh in by_right:
             ring_right[dzh].wait_recv()
             relays.append(move(-1, dzh, right))
         else:
@@ -334,10 +335,11 @@
             relays.append(move(1, dzh, left))
 
     def end():
-        for dzh in (0, 2):
-            ring_left[dzh].wait_recv()
-        for dzh in (1, 2, 3):
-            ring_right[dzh].wait_recv()
+        for dzh in range(4):
+            if dzh == 2 or dzh in by_right:
+                ring_left[dzh].wait_recv()
+            if dzh not in by_right:
+                ring_right[dzh].wait_recv()
         for made in relays:
             made.wait_recv()
 
@@ -554,7 +556,7 @@
         streams[f"r{half}"] = reduce_steps(
             around, send, parts[half], *[ref.at[half] for ref in reduce_scratch], results.at[half]
         )
-        streams[f"s{half}"] = spread_steps(around, send, backs[half])
+        streams[f"s{half}"] = spread_steps(around, send, backs[half], BY_RIGHT[half])
         streams[f"c{half}"] = scatter_steps(
             around, send, parts_back[half], grads.at[half],
             *[ref.at[half] for ref in scatter_scratch],

time: 107 us -> 105 us (0.981)
  Pallas kernels: 105 us -> 103 us
    pallas_call x1, Pallas kernels: 103 us -> 102 us  [layer(): pl.pallas_call(layer_kernel, out_shape=(jax.ShapeDtypeStruct((OWNED, WIDT...]
where the time goes in v4:
time: 105 us
  Pallas kernels  103 us (98%)
  between operations  1.29 us (1%)
    pallas_call x1, Pallas kernels, layer(): pl.pallas_call(layer_kernel, out_shape=(jax.ShapeDtypeStruct((OWNED, WIDT...  102 us

profile of v4, /device:TPU:1, one launch (start us, length us, event | category | flops | bytes accessed | tf_op | source)
XLA Modules:
  0.0 104.7 jit_solution(10582581462642155014)
XLA Ops:
  1.3 101.5 %layer.1 = (bf16[256,256]{1,0:T(8,128)(2,1)}, f32[256,256]{1,0:T(8,128)}, bf16[256,256]{1,0:T(8,128)(2,1)}) custom-call(s32[1]{0:T(128)} %bitcast.4.count, s32[1,192]{1,0:T(1,128)} %bitcast.6, s32[1,192]{1,0:T(1,128)} %bitcast.7, bf16[256,256]{1,0:T(8,128)(2,1)} %features.1, bf16[256,256]{1,0:T(8,128)(2,1)} %weight.1, bf16[256,256]{1,0:T(8,128)(2,1)} %cotangent.1, ...), custom_call_target="tpu_custom_call" | custom-call | tf_op jit(solution)/shard_map/layer/pallas_call | solution.py:631
  102.8 1.8 %hand_on.1 = (bf16[256,256]{1,0:T(8,128)(2,1)}, f32[256,256]{1,0:T(8,128)}, bf16[256,256]{1,0:T(8,128)(2,1)}) custom-call(bf16[256,256]{1,0:T(8,128)(2,1)} %get-tuple-element.6.refs_0_, f32[256,256]{1,0:T(8,128)} %get-tuple-element.7.refs_1_, bf16[256,256]{1,0:T(8,128)(2,1)} %get-tuple-element.8.refs_2_), custom_call_target="tpu_custom_call" | custom-call | tf_op jit(solution)/shard_map/hand_on/pallas_call | solution.py:679

commit v5 on v4

--- a/solution.py
+++ b/solution.py
@@ -28,8 +28,8 @@
 REDUCE_FIRST = ("r0.first0", "r0.first1", "r0.plain",)
 REDUCE_DURING = ((2,("r0.merge",)),)
 REDUCE_LAST = ("r0.late", "r0.last", "r1.first0", "r1.first1", "r1.plain", "r0.sum2", "r0.sum3", "r0.sum1", "r0.sum0", "r1.merge", "r1.late", "r1.last", "r0.end", "r1.sum2", "r1.sum3", "r1.sum1", "r1.sum0", "r1.end",)
-SPREAD_BEGIN = ("s0.begin", "s0.far", "s1.begin", "s1.far",)
-SPREAD_FIRST = ("w.weight0", "s0.relay0", "s1.relay0", "s0.level1", "s0.level2", "s0.level0", "s0.relay3", "s0.relay1", "w.weight1", "s1.level1", "s1.level2", "s1.level0", "w.weight2", "s0.end",)
+SPREAD_BEGIN = ("s0.begin", "s1.begin")
+SPREAD_FIRST = ("w.weight0", "s0.relay0", "s1.relay0", "s0.level1", "s0.level2", "s1.level1", "s1.level2", "s0.level0", "s0.relay3", "s0.relay1", "s1.level0", "w.weight1", "w.weight2", "s0.end")
 SPREAD_DURING = ((1,("s1.relay3",)),(2,("s1.relay1","w.weight3")))
 SPREAD_LAST = ("c0.cores", "s1.end", "w.weight4",)
 SCATTER_DURING = ((1,("c0.chips0","c0.chips1","w.weight5")),(2,("w.weight6",)))
@@ -317,11 +317,20 @@
         up[2] = move(0, 0, around.levels[2])
         ring(0)
 
-    def far():
-        up[0] = move(0, 0, around.levels[0])
+    def pass_on(dzh, tile, device):
+        def ends():
+            block = gathered.at[here.at(dzh=dzh)[1] * 2 + tile]
+            return block, block
+
+        return send.copy(ends, device)
 
     def level(slot):
-        up[slot].wait_recv()
+        if slot:
+            up[slot].wait_recv()
+            up[slot + 2] = pass_on(came[slot], slot - 1, around.levels[slot])
+        else:
+            up[3].wait_recv()
+            up[4].wait_recv()
         ring(came[slot])
         if slot == 0:
             relays.append(move(0, 2, around.beside[1]))
@@ -343,7 +352,7 @@
         for made in relays:
             made.wait_recv()
 
-    steps = {"begin": begin, "far": far, "end": end}
+    steps = {"begin": begin, "end": end}
     for slot in range(3):
         steps[f"level{slot}"] = functools.partial(level, slot)
     for dzh in (0, 1, 3):

time: 105 us -> 102 us (0.971)
  Pallas kernels: 103 us -> 101 us
    pallas_call x1, Pallas kernels: 102 us -> 99.1 us  [layer(): pl.pallas_call(layer_kernel, out_shape=(jax.ShapeDtypeStruct((OWNED, WIDT...]
where the time goes in v5:
time: 102 us
  Pallas kernels  101 us (99%)
  between operations  1.29 us (1%)
    pallas_call x1, Pallas kernels, layer(): pl.pallas_call(layer_kernel, out_shape=(jax.ShapeDtypeStruct((OWNED, WIDT...  99.1 us

profile of v5, /device:TPU:1, one launch (start us, length us, event | category | flops | bytes accessed | tf_op | source)
XLA Modules:
  0.0 102.2 jit_solution(2310203383484940540)
XLA Ops:
  1.3 99.1 %layer.1 = (bf16[256,256]{1,0:T(8,128)(2,1)}, f32[256,256]{1,0:T(8,128)}, bf16[256,256]{1,0:T(8,128)(2,1)}) custom-call(s32[1]{0:T(128)} %bitcast.4.count, s32[1,192]{1,0:T(1,128)} %bitcast.6, s32[1,192]{1,0:T(1,128)} %bitcast.7, bf16[256,256]{1,0:T(8,128)(2,1)} %features.1, bf16[256,256]{1,0:T(8,128)(2,1)} %weight.1, bf16[256,256]{1,0:T(8,128)(2,1)} %cotangent.1, ...), custom_call_target="tpu_custom_call" | custom-call | tf_op jit(solution)/shard_map/layer/pallas_call | solution.py:640
  100.4 1.8 %hand_on.1 = (bf16[256,256]{1,0:T(8,128)(2,1)}, f32[256,256]{1,0:T(8,128)}, bf16[256,256]{1,0:T(8,128)(2,1)}) custom-call(bf16[256,256]{1,0:T(8,128)(2,1)} %get-tuple-element.6.refs_0_, f32[256,256]{1,0:T(8,128)} %get-tuple-element.7.refs_1_, bf16[256,256]{1,0:T(8,128)(2,1)} %get-tuple-element.8.refs_2_), custom_call_target="tpu_custom_call" | custom-call | tf_op jit(solution)/shard_map/hand_on/pallas_call | solution.py:688
